TPU v7x, 512 devices: a whole 4x4x16 slice. The times are simulated.
512 devices in a mesh: row: 64 (over z_lo, x, y), col: 8 (over z_hi, core).
Axes of the slice: x: 4, y: 4, z: 16 (z_hi: 4, z_lo: 4; z = z_hi * 4 + z_lo), core: 2. Of those that a mesh axis runs over, the one named last changes fastest.
Arguments:
- features: bfloat16 [64, 32768], P(None, ('row', 'col')), may hold values from -6 to 6
- inv_scale: float32 [64], replicated, may hold values from 0.05 to 0.6
- pivots: int32 [64], replicated, may hold values from 0 to 32767, as said below
- solution: float32 [32, 32768], P(None, ('row', 'col')), may hold values from -6 to 6
- residual: float32 [32, 32768], P(None, ('row', 'col')), may hold values from -16 to 16
- direction: float32 [32, 32768], P(None, ('row', 'col')), may hold values from -16 to 16
Outputs:
- solution_out: float32 [32, 32768], P(None, ('row', 'col'))
- residual_out: float32 [32, 32768], P(None, ('row', 'col'))
- direction_out: float32 [32, 32768], P(None, ('row', 'col'))
- slope_image: float32 [32, 32768], P(None, ('row', 'col'))
Inputs may be any that keep to these rules, and one draw needn't show every extreme that they name: `pivots`: distinct; exactly one pivot in each aligned run of 512 samples, in no particular order.
All inputs are finite; a program needn't handle non-finite values.
Results may differ from a plain program's by a relative error of at most 0.019.
Values may be sent and summed in bfloat16 or wider, within the bound.
A program may use at most 64 MiB of HBM per device.

v0:
```python
import math

import jax
import jax.numpy as jnp
from jax import lax
from jax.sharding import PartitionSpec as P

noise_var = 1.0
highest = lax.Precision.HIGHEST


def scale_features(features, inv_scale):
    return (features.astype(jnp.float32) * inv_scale[:, None]).astype(jnp.bfloat16)


def square_norms(scaled):
    widened = scaled.astype(jnp.float32)
    return jnp.sum(widened * widened, axis=0)


def kernel_block(left, left_norm, right, right_norm):
    products = lax.dot_general(
        left, right, (((0,), (0,)), ((), ())), preferred_element_type=jnp.float32
    )
    distance = left_norm[:, None] + right_norm[None, :] - 2.0 * products
    return (jnp.exp(-0.5 * distance), distance)


def pick_block(count):
    if count <= 1024:
        return count
    return math.gcd(count, 512)


def tile_terms(accums, row_feat, row_norm, col_feat, col_dir):
    col_norm = square_norms(col_feat)
    row_count = row_feat.shape[1]
    col_count = col_feat.shape[1]
    row_block = pick_block(row_count)
    col_block = pick_block(col_count)
    columns = col_dir.shape[0]

    def row_step(row_index, totals):
        image_acc, slope_acc = totals
        row_slice = lax.dynamic_slice_in_dim(row_feat, row_index * row_block, row_block, 1)
        norm_slice = lax.dynamic_slice_in_dim(row_norm, row_index * row_block, row_block, 0)

        def col_step(col_index, partial_value):
            kernel_tile, distance = kernel_block(col_feat, col_norm, row_slice, norm_slice)
            kernel_half = kernel_tile.astype(jnp.bfloat16)
            slope_half = (kernel_tile * distance).astype(jnp.bfloat16)
            return (
                partial_value[0]
                + jnp.dot(col_dir, kernel_half, preferred_element_type=jnp.float32),
                partial_value[1] + jnp.dot(col_dir, slope_half, preferred_element_type=jnp.float32),
            )

        blank = jnp.zeros((columns, row_block), jnp.float32)
        kernel_part, slope_part = lax.fori_loop(0, col_count // col_block, col_step, (blank, blank))
        image_old = lax.dynamic_slice_in_dim(image_acc, row_index * row_block, row_block, 1)
        slope_old = lax.dynamic_slice_in_dim(slope_acc, row_index * row_block, row_block, 1)
        image_acc = lax.dynamic_update_slice_in_dim(
            image_acc, image_old + kernel_part, row_index * row_block, 1
        )
        slope_acc = lax.dynamic_update_slice_in_dim(
            slope_acc, slope_old + slope_part, row_index * row_block, 1
        )
        return (image_acc, slope_acc)

    return lax.fori_loop(0, row_count // row_block, row_step, accums)


def local(features, inv_scale, pivots, solution, residual, direction):
    scaled = scale_features(features, inv_scale)
    sq_norm = square_norms(scaled)
    own_count = scaled.shape[1]
    columns = direction.shape[0]
    dir_half = direction.astype(jnp.bfloat16)
    offset = lax.axis_index(("row", "col")) * own_count
    positions = offset + jnp.arange(own_count, dtype=jnp.int32)
    picks = (pivots[:, None] == positions[None, :]).astype(jnp.bfloat16)
    chosen = lax.dot_general(
        scaled, picks, (((1,), (1,)), ((), ())), preferred_element_type=jnp.float32
    )
    pivot_wide = lax.psum(chosen, ("row", "col"))
    pivot_feat = pivot_wide.astype(jnp.bfloat16)
    pivot_norm = square_norms(pivot_feat)
    own_kernel, unused_one = kernel_block(pivot_feat, pivot_norm, scaled, sq_norm)
    pivot_self, unused_two = kernel_block(pivot_feat, pivot_norm, pivot_feat, pivot_norm)
    gram_part = jnp.dot(own_kernel, own_kernel.T, precision=highest)
    proj_part = jnp.dot(residual, own_kernel.T, precision=highest)
    square_part = jnp.sum(residual * residual, axis=1)
    gram_sum, proj_old, square_old = lax.psum((gram_part, proj_part, square_part), ("row", "col"))
    gram = noise_var * pivot_self + gram_sum
    factor = jnp.linalg.cholesky(gram)
    solved_old = jax.scipy.linalg.cho_solve((factor, True), proj_old.T)
    norm_old = (square_old - jnp.sum(proj_old.T * solved_old, axis=0)) / noise_var
    row_feat = lax.all_gather(scaled, "row", axis=1, tiled=True)
    row_norm = square_norms(row_feat)
    blank = jnp.zeros((columns, row_feat.shape[1]), jnp.float32)
    totals = tile_terms(
        (blank, blank),
        row_feat,
        row_norm,
        lax.all_gather(scaled, "col", axis=1, tiled=True),
        lax.all_gather(dir_half, "col", axis=1, tiled=True),
    )
    kernel_image, slope_image = (
        lax.psum_scatter(totals[0], "row", scatter_dimension=1, tiled=True),
        lax.psum_scatter(totals[1], "row", scatter_dimension=1, tiled=True),
    )
    image = kernel_image + noise_var * direction
    curvature = lax.psum(jnp.sum(direction * image, axis=1), ("row", "col"))
    step_size = norm_old / curvature
    solution_out = solution + step_size[:, None] * direction
    residual_out = residual - step_size[:, None] * image
    proj_new = lax.psum(jnp.dot(residual_out, own_kernel.T, precision=highest), ("row", "col"))
    solved_new = jax.scipy.linalg.cho_solve((factor, True), proj_new.T)
    precond_new = (residual_out - jnp.dot(solved_new.T, own_kernel, precision=highest)) / noise_var
    norm_new = lax.psum(jnp.sum(residual_out * precond_new, axis=1), ("row", "col"))
    direction_out = precond_new + (norm_new / norm_old)[:, None] * direction
    return (solution_out, residual_out, direction_out, slope_image)


def solution(mesh):
    placed = (
        P(None, ("row", "col")),
        P(),
        P(),
        P(None, ("row", "col")),
        P(None, ("row", "col")),
        P(None, ("row", "col")),
    )
    return jax.shard_map(
        local,
        mesh=mesh,
        in_specs=placed,
        out_specs=(
            P(None, ("row", "col")),
            P(None, ("row", "col")),
            P(None, ("row", "col")),
            P(None, ("row", "col")),
        ),
        check_vma=False,
    )
```

profile of v0, /device:TPU:128, one launch (start us, length us, event | category | flops | bytes accessed | tf_op | source)
XLA Modules:
  0.0 1012.5 jit_solution(14300741523737838248)
XLA Ops:
  7.2 0.8 copy.22
  8.0 0.8 multiply_reduce_fusion.2
  8.8 21.8 %all_gather.9 = bf16[64,512]{0,1:T(8,128)(2,1)S(1)} all-gather(bf16[64,64]{0,1:T(8,128)(2,1)S(1)} %get-tuple-element.228), channel_id=1, replica_groups=mesh['row'=64,'col'=8] {'col'}, dimensions={1}, use_global_device_ids=true | all-gather | bytes 73728 | tf_op jit(solution)/shard_map/all_gather | solution.py:105
  30.6 191.1 %all_gather.10 = bf16[64,4096]{0,1:T(8,128)(2,1)S(1)} all-gather(bf16[64,64]{0,1:T(8,128)(2,1)S(1)} %get-tuple-element.228), channel_id=1, replica_groups=mesh['row'=64,'col'=8] {'row'}, dimensions={1}, use_global_device_ids=true | all-gather | bytes 532480 | tf_op jit(solution)/shard_map/all_gather | solution.py:98
  221.7 0.6 multiply_reduce_fusion
  222.9 18.1 %all-gather = bf16[8,64,32]{1,2,0:T(8,128)(2,1)S(1)} all-gather(bf16[1,64,32]{1,2,0:T(8,128)(2,1)S(1)} %convert_bitcast_fusion), channel_id=1, replica_groups=mesh['row'=64,'col'=8] {'col'}, dimensions={0}, use_global_device_ids=true | all-gather | bytes 36864 | tf_op jit(solution)/shard_map/all_gather | solution.py:106
  241.3 8.0 while.26
  245.4 0.3 fusion.74
  247.4 0.3 fusion.74
  249.3 2.0 copy.33
  251.3 1.9 copy.35
  253.5 99.9 %psum.50 = bf16[64,64]{1,0:T(8,128)(2,1)S(1)} all-reduce(f32[64,64]{1,0:T(8,128)S(1)} %fusion.31), channel_id=1, replica_groups=mesh['row'=64,'col'=8] {'row','col'}, use_global_device_ids=true, to_apply=%region_2.0 | all-reduce | flops 4096 | bytes 24576 | tf_op jit(solution)/shard_map/psum | solution.py:85
  353.9 272.2 %reduce-scatter.7.cloned.1.call-done = f32[64,32]{1,0:T(8,128)} async-done(((f32[4096,32]{1,0:T(8,128)}), f32[64,32]{1,0:T(8,128)}) %reduce-scatter.7.cloned.1.call-update) | async-done | bytes 8208
  626.1 0.8 copy.34
  627.1 98.5 %all-reduce = (f32[32]{0:T(128)S(1)}, f32[64,32]{0,1:T(8,128)S(1)}, f32[64,64]{0,1:T(8,128)S(1)}, f32[32]{0:T(128)S(1)}) all-reduce(f32[32]{0:T(128)S(1)} %get-tuple-element.233, f32[64,32]{0,1:T(8,128)S(1)} %fusion.38, f32[64,64]{0,1:T(8,128)S(1)} %fusion.39, ...), channel_id=1, replica_groups=mesh['row'=64,'col'=8] {'row','col'}, use_global_device_ids=true, to_apply=%region_1.0 | all-reduce | flops 6208 | bytes 49664 | tf_op jit(solution)/shard_map/psum | solution.py:93
  725.9 5.8 cholesky.18
  731.8 0.6 compare_reduce_fusion
  732.4 0.7 fusion.22
  733.1 4.9 custom-call.9
  738.7 101.7 %psum.54 = f32[64,32]{0,1:T(8,128)S(1)} all-reduce(f32[64,32]{0,1:T(8,128)S(1)} %fusion.40), channel_id=1, replica_groups=mesh['row'=64,'col'=8] {'row','col'}, use_global_device_ids=true, to_apply=%region_17.19 | all-reduce | flops 2048 | bytes 16384 | tf_op jit(solution)/shard_map/psum | solution.py:117
  841.0 100.3 %psum.55 = f32[32]{0:T(128)S(1)} all-reduce(f32[32]{0:T(128)S(1)} %get-tuple-element.231), channel_id=1, replica_groups=mesh['row'=64,'col'=8] {'row','col'}, use_global_device_ids=true, to_apply=%region_19.21 | all-reduce | flops 32 | bytes 256 | tf_op jit(solution)/shard_map/psum | solution.py:120
  941.2 62.3 %reduce-scatter.9.cloned.1.call-done = f32[64,32]{1,0:T(8,128)} async-done(((f32[4096,32]{1,0:T(8,128)}), f32[64,32]{1,0:T(8,128)}) %reduce-scatter.9.cloned.1.call-update) | async-done | bytes 8208
  1003.5 1.4 copy.36
  1005.0 0.7 multiply_add_fusion
  (72 shorter events, 10.6 us)
Async XLA Ops:
  7.2 619.0 %reduce-scatter.7.cloned.1.call-start = ((), (), s32[]{:S(2)}) async-start(), calls=%async_computation.2 | async-start | bytes 2129920
  8.8 214.1 %copy-start.2 = (f32[32,64]{1,0:T(8,128)S(1)}, f32[32,64]{1,0:T(8,128)}, u32[]{:S(2)}) copy-start(f32[32,64]{1,0:T(8,128)} %param.15) | copy-start | bytes 24580
  251.3 752.2 %reduce-scatter.9.cloned.1.call-start = ((), (), s32[]{:S(2)}) async-start(), calls=%async_computation.3 | async-start | bytes 2129920
  251.3 2.0 copy-start.4
  251.3 102.4 %copy-start.1 = (f32[32,64]{1,0:T(8,128)S(1)}, f32[32,64]{1,0:T(8,128)}, u32[]{:S(2)}) copy-start(f32[32,64]{1,0:T(8,128)} %param.14) | copy-start | bytes 24580
  253.3 751.7 %copy-start.3 = (f32[32,64]{1,0:T(8,128)S(1)}, f32[32,64]{1,0:T(8,128)}, u32[]{:S(2)}) copy-start(f32[32,64]{1,0:T(8,128)} %param.13) | copy-start | bytes 24580
  738.5 267.1 %copy-start = (f32[32,64]{1,0:T(8,128)}, f32[32,64]{1,0:T(8,128)S(1)}, u32[]{:S(2)}) copy-start(f32[32,64]{1,0:T(8,128)S(1)} %multiply_subtract_fusion) | copy-start | bytes 24580
Sparse Core Ops, SparseCore 0:
  251.4 374.6 reduce-scatter.6
  629.1 374.3 reduce-scatter.8
where the time goes:
time: 1010 us
  blocking collectives  631 us (62%)
  waiting for transfers between devices  334 us (33%)
  other arithmetic  14.5 us (1%)
  between operations  14.3 us (1%)
    unnamed x4, waiting for transfers between devices  334 us
    all_gather x1, blocking collectives, local(): row_feat = lax.all_gather(scaled, 'row', axis=1, tiled=True)  191 us
    psum x1, blocking collectives, local(): lax.psum(jnp.dot(residual_out, own_kernel.T, precision=highest), ('row',...  102 us
    psum x1, blocking collectives, local(): lax.psum(jnp.sum(residual_out * precond_new, axis=1), ('row', 'col'))  100 us
    psum x1, blocking collectives, local(): pivot_wide = lax.psum(chosen, ('row', 'col'))  99.9 us
    psum x1, blocking collectives, local(): lax.psum((gram_part, proj_part, square_part), ('row', 'col'))  98.5 us
    all_gather x1, blocking collectives, local(): lax.all_gather(scaled, 'col', axis=1, tiled=True)  21.8 us
  transfers between devices with their start and end apart: 2, of which 2 were waited for; matrix products, arithmetic and copies ran while one was open for 2% of the time, Pallas kernels for 0%

commit v1 on v0

v1 whole, which is shorter than its diff:
```python
import jax
import jax.numpy as jnp
from jax import lax
from jax.experimental import pallas as pl
from jax.experimental.pallas import tpu as pltpu
from jax.sharding import PartitionSpec as P

noise_var = 1.0
MESH = pl.DeviceIdType.MESH
highest = lax.Precision.HIGHEST
f32 = jnp.float32
bf16 = jnp.bfloat16
NT = (((1,), (1,)), ((), ()))
NN = (((1,), (0,)), ((), ()))


def iota(shape, dim):
    return lax.broadcasted_iota(jnp.int32, shape, dim)


def pieces(norm):
    high = norm.astype(bf16).astype(f32)
    rest = norm - high
    mid = rest.astype(bf16).astype(f32)
    low = (rest - mid).astype(bf16).astype(f32)
    return high, mid, low


def with_norms(values, lane):
    norm = jnp.sum(values * values, axis=1, keepdims=True)
    high, mid, low = pieces(norm)
    values = values + jnp.where((lane == 32) | (lane == 35), high, 0.0)
    values = values + jnp.where((lane == 33) | (lane == 36), mid, 0.0)
    return values + jnp.where((lane == 34) | (lane == 37), low, 0.0)


def lane_rows():
    lane = iota((1, 128), 1)
    feat = lane >= 64
    first = (lane >= 32) & (lane < 35)
    second = (lane >= 35) & (lane < 38)
    one = jnp.where(first | feat, 1.0, 0.0)
    col_scale = one.astype(bf16)
    col_shift = jnp.where(second, 1.0, 0.0).astype(bf16)
    row_scale = jnp.where(feat, -2.0, jnp.where(second, 1.0, 0.0)).astype(bf16)
    row_shift = jnp.where(first, 1.0, 0.0).astype(bf16)
    return col_scale, col_shift, row_scale, row_shift


def kernel(
    feat_hbm, inv_hbm, piv_hbm, sol_hbm, res_hbm, dir_hbm,
    sol_out, res_out, dir_out, slope_out,
    feat_in, inv_in, piv_in, sol_in, res_in, dir_in,
    stage_a, stage_b,
    zbuf, xbuf, colm, wmat,
    fold, fold_sib, part, part_xy,
    q_own, q_sib, q_sum, q_xy,
    g_own, g_sib, g_sum, g_xy,
    p_own, p_sib, p_sum, p_xy, p_tot, p_z, p_half, p_other,
    in_sem, zs, zr, xs, xr, ws, wr, fs, fr, ps, pr, qs, qr, qxs, qxr, gs, gr, gxs, gxr, ts, tr, txs, txr, tzs, tzr, us, ur,
):
    row = lax.axis_index("row")
    col = lax.axis_index("col")
    xy = lax.rem(row, 16)
    core = lax.rem(col, 2)
    z = (col // 2) * 4 + row // 16

    def dev(z_at, xy_at, core_at):
        return (lax.rem(z_at, 4) * 16 + xy_at, (z_at // 4) * 2 + core_at)

    def z_peer(k):
        far = 8 - (k + 1) // 2
        return lax.rem(z + jnp.where(lax.rem(k, 2) == 1, far, 16 - far), 16)

    def xy_peer(k):
        return lax.rem(xy + k, 16)

    sibling = dev(z, xy, 1 - core)

    def remote(src, dst, send, recv, where):
        return pltpu.make_async_remote_copy(
            src_ref=src, dst_ref=dst, send_sem=send, recv_sem=recv, device_id=where, device_id_type=MESH
        )

    def loop(low, high, body):
        def step(k, carry):
            body(k)
            return carry

        lax.fori_loop(low, high, step, 0)

    barrier = pltpu.get_barrier_semaphore()

    def greet(where):
        pl.semaphore_signal(barrier, inc=1, device_id=where, device_id_type=MESH)

    loop(0, 15, lambda k: greet(dev(z_peer(k), xy, core)))
    loop(1, 16, lambda k: greet(dev(z, xy_peer(k), core)))
    greet(sibling)

    loads = [
        pltpu.make_async_copy(src, dst, in_sem.at[n])
        for n, (src, dst) in enumerate(
            (
                (feat_hbm, feat_in), (inv_hbm, inv_in), (piv_hbm, piv_in),
                (sol_hbm, sol_in), (res_hbm, res_in), (dir_hbm, dir_in),
            )
        )
    ]
    for load in loads:
        load.start()
    stage_a[...] = jnp.zeros((128, 128), f32)
    stage_b[...] = jnp.zeros((128, 128), f32)
    for load in loads:
        load.wait()

    lane = iota((64, 128), 1)
    line = iota((64, 128), 0)
    stage_a[0:32, 0:64] = dir_in[...]
    stage_a[64:128, 0:64] = feat_in[...].astype(f32)
    stage_b[0:32, 0:64] = res_in[...]
    stage_b[32:64, 0:64] = sol_in[...]
    turned = stage_a[...].T[0:64]
    others = stage_b[...].T[0:64]
    dir_t = jnp.where(lane < 32, turned, 0.0)
    res_t = jnp.where(lane < 32, others, 0.0)
    sol_t = jnp.where(lane < 32, pltpu.roll(others, 96, 1), 0.0)
    stage_a[0:1, 0:64] = inv_in[...]
    stage_a[0:1, 64:128] = jnp.zeros((1, 64), f32)
    inv_row = pltpu.roll(stage_a[0:8, :], 64, 1)[0:1]
    scaled = jnp.where(lane >= 64, (turned * inv_row).astype(bf16).astype(f32), 0.0)

    offset = (row * 8 + col) * 64
    hits = piv_in[...] == iota((64, 64), 0) + offset
    picked = jnp.max(jnp.where(hits, 1.0, 0.0), axis=1, keepdims=True)
    chosen = jnp.broadcast_to(jnp.sum(picked * scaled, axis=0, keepdims=True), (8, 128))
    block = with_norms(scaled, lane) + dir_t
    for k in range(4):
        moved = pltpu.roll(chosen, (38 - 64 - 16 * k) % 128, 1)[0:1]
        block = block + jnp.where((line == k) & (lane >= 38) & (lane < 54), moved, 0.0)
    own = block.astype(bf16)
    zbuf[z] = own
    xbuf[core, xy] = own

    pl.semaphore_wait(barrier, 31)

    def z_copy(k):
        return remote(zbuf.at[z], zbuf.at[z], zs.at[k], zr.at[z], dev(z_peer(k), xy, core))

    def x_copy(k):
        return remote(xbuf.at[core, xy], xbuf.at[core, xy], xs.at[k], xr.at[xy], dev(z, xy_peer(k), core))

    def w_copy(p):
        return remote(xbuf.at[core, p], xbuf.at[core, p], ws.at[p], wr.at[p], sibling)

    loop(0, 15, lambda k: z_copy(k).start())
    loop(1, 16, lambda k: x_copy(k).start())
    w_copy(xy).start()

    def forward(k):
        p = xy_peer(k)
        remote(xbuf.at[core, p], xbuf.at[core, p], xs.at[k], xr.at[p], sibling).wait_recv()
        w_copy(p).start()

    loop(1, 16, forward)

    def z_arrive(k):
        p = z_peer(k)
        remote(zbuf.at[p], zbuf.at[p], zs.at[k], zr.at[p], sibling).wait_recv()

    loop(0, 15, z_arrive)

    lane16 = iota((16, 128), 1)
    line16 = iota((16, 128), 0)
    found = jnp.zeros((16, 128), f32)
    for low in range(4):
        seen = zbuf[low, 0:16, :].astype(f32)
        for high in range(1, 4):
            seen = seen + zbuf[high * 4 + low, 0:16, :].astype(f32)
        seen = jnp.where((lane16 >= 38) & (lane16 < 54), seen, 0.0)[0:8]
        whole = jnp.zeros((1, 128), f32)
        for k in range(4):
            whole = whole + pltpu.roll(seen, 64 + 16 * k - 38, 1)[k : k + 1]
        found = found + jnp.where(line16 == lax.rem(xy, 4) * 4 + low, whole, 0.0)
    q_own[...] = found.astype(bf16)
    q_copy = remote(q_own, q_sib, qs, qr, sibling)
    q_copy.start()

    col_scale, col_shift, row_scale, row_shift = lane_rows()
    lane_w = iota((64, 128), 1)

    def columns(k):
        held = zbuf[k]
        start = pl.multiple_of(k * 64, 64)
        colm[pl.ds(start, 64), :] = held * col_scale + col_shift
        direction = jnp.where(lane_w < 32, held.astype(f32), 0.0)
        wmat[0, pl.ds(start, 64), :] = direction.astype(bf16)
        wmat[1, pl.ds(start, 64), :] = pltpu.roll(direction, 32, 1).astype(bf16)

    loop(0, 16, columns)

    def tile(owner, chunk):
        rows = xbuf[owner, pl.ds(chunk * 4, 4)].reshape(256, 128) * row_scale + row_shift
        total = jnp.zeros((256, 128), f32)
        for part_at in range(4):
            cols = slice(part_at * 256, part_at * 256 + 256)
            distance = lax.dot_general(rows, colm[cols, :], NT, preferred_element_type=f32)
            value = jnp.exp(-0.5 * distance)
            total = total + jnp.dot(value.astype(bf16), wmat[0, cols, :], preferred_element_type=f32)
            total = total + jnp.dot((value * distance).astype(bf16), wmat[1, cols, :], preferred_element_type=f32)
        total = total.reshape(4, 64, 128)
        upper = total[:, 0:32].reshape(128, 128)
        lower = total[:, 32:64].reshape(128, 128)
        fold[owner, pl.ds(chunk * 4, 4)] = (upper + pltpu.roll(lower, 64, 1)).reshape(4, 32, 128)

    def w_arrive(p):
        remote(xbuf.at[1 - core, p], xbuf.at[1 - core, p], ws.at[p], wr.at[p], sibling).wait_recv()

    loop(0, 16, w_arrive)
    loop(0, 4, lambda chunk: tile(1 - core, chunk))
    f_copy = remote(fold.at[1 - core], fold_sib, fs, fr, sibling)
    f_copy.start()

    q_copy.wait()
    q_sum[...] = (q_own[...].astype(f32) + q_sib[...].astype(f32)).astype(bf16)
    q_xy[xy] = q_sum[...]

    def q_send(k):
        return remote(q_sum, q_xy.at[xy], qxs.at[k], qxr.at[xy], dev(z, xy_peer(k), core))

    loop(1, 16, lambda k: q_send(k).start())

    loop(0, 4, lambda chunk: tile(core, chunk))
    f_copy.wait()
    part[...] = fold[core] + fold_sib[...]
    part_xy[xy] = part[xy]

    def s_copy(k):
        p = xy_peer(k)
        return remote(part.at[p], part_xy.at[xy], ps.at[k], pr.at[xy], dev(z, p, core))

    loop(1, 16, lambda k: s_copy(k).start())

    def q_arrive(k):
        p = xy_peer(k)
        remote(q_xy.at[p], q_xy.at[p], qxs.at[k], qxr.at[p], sibling).wait_recv()

    loop(1, 16, q_arrive)
    lots = []
    for x_at in range(4):
        lot = q_xy[x_at * 4].astype(f32)
        for y_at in range(1, 4):
            lot = lot + q_xy[x_at * 4 + y_at].astype(f32)
        lots.append(lot)
    pivot = with_norms(jnp.concatenate(lots, axis=0), lane).astype(bf16)
    pivot_row = pivot * row_scale + row_shift
    pivot_col = pivot * col_scale + col_shift

    def kern(left, right):
        return jnp.exp(-0.5 * lax.dot_general(left, right, NT, preferred_element_type=f32))

    def exact(left, right, numbers):
        return lax.dot_general(left, right, numbers, precision=highest, preferred_element_type=f32)

    line_kernel = kern(pivot_row, colm[...])
    gram_part = exact(line_kernel, line_kernel, NT)
    wide = jnp.concatenate([gram_part, jnp.zeros((64, 64), f32)], axis=1)
    g_own[...] = wide[0:32] + pltpu.roll(wide[32:64], 64, 1)
    g_copy = remote(g_own, g_sib, gs, gr, sibling)
    g_copy.start()
    own_col = own * col_scale + col_shift
    own_row = own * row_scale + row_shift
    own_kernel = kern(pivot_row, own_col)
    own_kernel_t = kern(own_row, pivot_col)
    pivot_self = kern(pivot_row, pivot_col)
    g_copy.wait()
    g_sum[...] = g_own[...] + g_sib[...]
    g_xy[xy] = g_sum[...]

    def g_send(k):
        return remote(g_sum, g_xy.at[xy], gxs.at[k], gxr.at[xy], dev(z, xy_peer(k), core))

    loop(1, 16, lambda k: g_send(k).start())

    def s_arrive(k):
        p = xy_peer(k)
        remote(part.at[p], part_xy.at[p], ps.at[k], pr.at[p], sibling).wait_recv()

    loop(1, 16, s_arrive)
    folded = jnp.sum(part_xy[...], axis=0)
    images = jnp.concatenate([folded, pltpu.roll(folded, 64, 1)], axis=0)
    image = jnp.where(lane < 32, images + noise_var * dir_t, 0.0)
    slope = jnp.where((lane >= 32) & (lane < 64), images, 0.0)
    both = image + pltpu.roll(res_t, 32, 1)
    proj = exact(own_kernel, both, NN)
    p_own[0:32, :] = proj[0:32] + pltpu.roll(proj[32:64], 64, 1)
    line8 = iota((8, 128), 0)
    sums = jnp.zeros((8, 128), f32)
    for n, value in enumerate((dir_t * image, res_t * image, image * image, res_t * res_t)):
        sums = sums + jnp.where(line8 == n, jnp.sum(value, axis=0, keepdims=True), 0.0)
    p_own[32:40, :] = sums
    p_copy = remote(p_own, p_sib, ts, tr, sibling)
    p_copy.start()
    p_copy.wait()
    p_sum[...] = p_own[...] + p_sib[...]
    p_xy[xy] = p_sum[...]

    def p_send(k):
        return remote(p_sum, p_xy.at[xy], txs.at[k], txr.at[xy], dev(z, xy_peer(k), core))

    loop(1, 16, lambda k: p_send(k).start())

    def p_arrive(k):
        p = xy_peer(k)
        remote(p_xy.at[p], p_xy.at[p], txs.at[k], txr.at[p], sibling).wait_recv()

    loop(1, 16, p_arrive)
    p_tot[...] = jnp.sum(p_xy[...], axis=0)
    half = pl.multiple_of(core * 16, 8)
    p_z[z] = p_tot[pl.ds(half, 24), :]

    def t_send(k):
        return remote(p_z.at[z], p_z.at[z], tzs.at[k], tzr.at[z], dev(z_peer(k), xy, core))

    loop(0, 15, lambda k: t_send(k).start())

    def g_arrive(k):
        p = xy_peer(k)
        remote(g_xy.at[p], g_xy.at[p], gxs.at[k], gxr.at[p], sibling).wait_recv()

    loop(1, 16, g_arrive)
    gathered = jnp.sum(g_xy[...], axis=0)
    gram = jnp.concatenate([gathered, pltpu.roll(gathered, 64, 1)], axis=0)
    own_self = jnp.concatenate([noise_var * pivot_self, jnp.zeros((64, 64), f32)], axis=1)
    work = jnp.where(lane < 64, gram + own_self, jnp.where(lane == line + 64, 1.0, 0.0))
    for k in range(64):
        head = work[k : k + 1, :]
        factor = work[:, k : k + 1] * (1.0 / head[:, k : k + 1])
        work = work - jnp.where(line > k, factor, 0.0) * head
    pivots_d = jnp.sum(jnp.where(lane == line, work, 0.0), axis=1, keepdims=True)
    lower_inv = pltpu.roll(work, 64, 1)[:, 0:64] * lax.rsqrt(pivots_d)
    gram_inv = exact(lower_inv.T, lower_inv, NN)
    mapped = exact(own_kernel_t, gram_inv, NN)

    def t_arrive(k):
        p = z_peer(k)
        remote(p_z.at[p], p_z.at[p], tzs.at[k], tzr.at[p], sibling).wait_recv()

    loop(0, 15, t_arrive)
    p_half[...] = jnp.sum(p_z[...], axis=0)
    u_copy = remote(p_half, p_other, us, ur, sibling)
    u_copy.start()
    u_copy.wait()
    mine = p_half[...]
    other = p_other[...]
    top = jnp.where(core == 0, mine, other)
    bottom = jnp.where(core == 0, other, mine)
    packed = jnp.concatenate([top, bottom[8:16]], axis=0)
    scalars = bottom[16:24]

    projs = jnp.concatenate([packed, pltpu.roll(packed, 64, 1)], axis=0)
    solved = exact(gram_inv, projs, NN)
    spread = exact(mapped, projs, NN)

    def old(values):
        return pltpu.roll(values, 96, 1)

    curvature = scalars[0:1]
    cross = scalars[1:2]
    square = scalars[2:3]
    square_old = scalars[3:4]
    proj_old = old(projs)
    solved_old = old(solved)
    norm_old = (square_old - jnp.sum(proj_old * solved_old, axis=0, keepdims=True)) / noise_var
    step = norm_old / curvature
    solution_new = sol_t + step * dir_t
    residual_new = res_t - step * image
    proj_new = proj_old - step * projs
    solved_new = solved_old - step * solved
    square_new = square_old - 2.0 * step * cross + step * step * square
    norm_new = (square_new - jnp.sum(proj_new * solved_new, axis=0, keepdims=True)) / noise_var
    precond_new = (residual_new - (old(spread) - step * spread)) / noise_var
    direction_new = precond_new + (norm_new / norm_old) * dir_t

    result = jnp.where(
        lane < 32,
        solution_new,
        jnp.where(
            lane < 64,
            pltpu.roll(residual_new, 32, 1),
            jnp.where(lane < 96, pltpu.roll(direction_new, 64, 1), pltpu.roll(slope, 64, 1)),
        ),
    )
    stage_b[0:64, :] = result
    turned_back = stage_b[...].T
    sol_out[...] = turned_back[0:32, 0:64]
    res_out[...] = turned_back[32:64, 0:64]
    dir_out[...] = turned_back[64:96, 0:64]
    slope_out[...] = turned_back[96:128, 0:64]

    loop(0, 15, lambda k: z_copy(k).wait_send())
    loop(1, 16, lambda k: x_copy(k).wait_send())
    loop(0, 16, lambda p: w_copy(p).wait_send())
    loop(1, 16, lambda k: q_send(k).wait_send())
    loop(1, 16, lambda k: s_copy(k).wait_send())
    loop(1, 16, lambda k: g_send(k).wait_send())
    loop(1, 16, lambda k: p_send(k).wait_send())
    loop(0, 15, lambda k: t_send(k).wait_send())


def local(features, inv_scale, pivots, solution, residual, direction):
    vmem = pltpu.VMEM
    dma = pltpu.SemaphoreType.DMA
    one = dma(())
    many = dma((16,))
    shape = jax.ShapeDtypeStruct((32, 64), f32)
    scratch = [
        vmem((64, 64), bf16), vmem((1, 64), f32), vmem((1, 64), jnp.int32),
        vmem((32, 64), f32), vmem((32, 64), f32), vmem((32, 64), f32),
        vmem((128, 128), f32), vmem((128, 128), f32),
        vmem((16, 64, 128), bf16), vmem((2, 16, 64, 128), bf16), vmem((1024, 128), bf16), vmem((2, 1024, 128), bf16),
        vmem((2, 16, 32, 128), f32), vmem((16, 32, 128), f32), vmem((16, 32, 128), f32), vmem((16, 32, 128), f32),
        vmem((16, 128), bf16), vmem((16, 128), bf16), vmem((16, 128), bf16), vmem((16, 16, 128), bf16),
        vmem((32, 128), f32), vmem((32, 128), f32), vmem((32, 128), f32), vmem((16, 32, 128), f32),
        vmem((40, 128), f32), vmem((40, 128), f32), vmem((40, 128), f32), vmem((16, 40, 128), f32),
        vmem((40, 128), f32), vmem((16, 24, 128), f32), vmem((24, 128), f32), vmem((24, 128), f32),
        dma((6,)),
        many, many, many, many, many, many, one, one, many, many, one, one, many, many,
        one, one, many, many, one, one, many, many, many, many, one, one,
    ]
    return pl.pallas_call(
        kernel,
        name="cg_step",
        out_shape=(shape,) * 4,
        in_specs=[pl.BlockSpec(memory_space=pl.ANY)] * 6,
        out_specs=(pl.BlockSpec(memory_space=pltpu.VMEM),) * 4,
        scratch_shapes=scratch,
        compiler_params=pltpu.CompilerParams(
            collective_id=0, has_side_effects=True, vmem_limit_bytes=40 * 1024 * 1024
        ),
    )(features, inv_scale[None, :], pivots[None, :], solution, residual, direction)


def solution(mesh):
    placed = (
        P(None, ("row", "col")),
        P(),
        P(),
        P(None, ("row", "col")),
        P(None, ("row", "col")),
        P(None, ("row", "col")),
    )
    return jax.shard_map(
        local,
        mesh=mesh,
        in_specs=placed,
        out_specs=(P(None, ("row", "col")),) * 4,
        check_vma=False,
    )
```

time: 1010 us -> 77.2 us (0.08)
  the two profiles are of different devices: /device:TPU:128 before, /device:TPU:1 now
where the time goes in v1:
time: 77.2 us; the launch traced here: 76.7 us
  Pallas kernels  70.1 us (91%)
  local copies, waits for them, and re-layouts  5.95 us (8%)
    pallas_call x1, Pallas kernels, local(): pl.pallas_call(kernel, name='cg_step', out_shape=(shape,) * 4, in_specs=[...  70.1 us
    unnamed x16, local copies, waits for them, and re-layouts  5.95 us

profile of v1, /device:TPU:1, one launch (start us, length us, event | category | flops | bytes accessed | tf_op | source)
XLA Modules:
  0.0 76.7 jit_solution(7560378251731152604)
XLA Ops:
  0.6 0.0 copy-start.4
  0.6 0.0 copy-start.5
  0.7 0.6 copy-done.4
  1.3 0.0 copy-done.5
  1.3 0.0 copy-start
  1.3 0.7 copy-done
  2.0 0.0 copy-start.1
  2.0 0.7 copy-done.1
  2.7 0.0 copy-start.2
  2.7 0.7 copy-done.2
  3.5 0.0 copy-start.3
  3.5 0.7 copy-done.3
  4.2 70.1 %cg_step.1 = (f32[32,64]{1,0:T(8,128)S(1)}, f32[32,64]{1,0:T(8,128)S(1)}, f32[32,64]{1,0:T(8,128)S(1)}, f32[32,64]{1,0:T(8,128)S(1)}) custom-call(bf16[64,64]{1,0:T(8,128)(2,1)S(1)} %copy-done, f32[1,64]{1,0:T(1,128)S(1)} %bitcast.2, s32[1,64]{1,0:T(1,128)S(1)} %bitcast.3, f32[32,64]{1,0:T(8,128)S(1)} %copy-done.1, f32[32,64]{1,0:T(8,128)S(1)} %copy-done.2, ...), custom_call_target="tpu_custom_call" | custom-call | tf_op jit(solution)/shard_map/cg_step/pallas_call | solution.py:431
  74.3 0.6 copy.14
  74.9 0.6 copy.15
  75.5 0.6 copy.16
  76.1 0.6 copy.17
Async XLA Ops:
  0.6 0.7 copy-start.4
  0.6 0.7 copy-start.5
  1.3 0.7 copy-start
  2.0 0.7 copy-start.1
  2.7 0.7 copy-start.2
  3.5 0.7 copy-start.3

commit v2 on v1

v2 whole, which is shorter than its diff:
```python
import jax
import jax.numpy as jnp
from jax import lax
from jax.experimental import pallas as pl
from jax.experimental.pallas import tpu as pltpu
from jax.sharding import PartitionSpec as P

noise_var = 1.0
MESH = pl.DeviceIdType.MESH
highest = lax.Precision.HIGHEST
f32 = jnp.float32
bf16 = jnp.bfloat16
NT = (((1,), (1,)), ((), ()))
NN = (((1,), (0,)), ((), ()))


def iota(shape, dim):
    return lax.broadcasted_iota(jnp.int32, shape, dim)


def loop(low, high, body):
    def step(k, carry):
        body(k)
        return carry

    lax.fori_loop(low, high, step, 0)


def exact(left, right, numbers=NN):
    return lax.dot_general(left, right, numbers, precision=highest, preferred_element_type=f32)


def kernel_of(left, right):
    return jnp.exp(lax.dot_general(left, right, NT, preferred_element_type=f32))


def forms(scaled, lane):
    norm = jnp.sum(scaled * scaled, axis=1, keepdims=True)
    high = norm.astype(bf16).astype(f32)
    rest = norm - high
    mid = rest.astype(bf16).astype(f32)
    low = (rest - mid).astype(bf16).astype(f32)
    place = lane - 32
    first = jnp.where(place == 0, high, jnp.where(place == 1, mid, jnp.where(place == 2, low, 0.0)))
    place = lane - 35
    second = jnp.where(place == 0, high, jnp.where(place == 1, mid, jnp.where(place == 2, low, 0.0)))
    in_first = (lane >= 32) & (lane < 35)
    in_second = (lane >= 35) & (lane < 38)
    row_form = scaled + second + jnp.where(in_first, -0.5, 0.0)
    col_form = scaled + first + jnp.where(in_second, -0.5, 0.0)
    return row_form, col_form


def unfold(packed):
    return jnp.concatenate([packed, pltpu.roll(packed, 64, 1)], axis=0)


def step_kernel(
    feat_hbm, inv_hbm, piv_hbm, sol_hbm, res_hbm, dir_hbm,
    result,
    feat_in, inv_in, piv_in, sol_in, res_in, dir_in,
    stage_a, stage_b,
    zbuf, xbuf, weights, acc,
    fold, fold_sib, part, part_xy,
    q_z,
    g_own, g_sib, g_sum, g_xy,
    l_own, l_sib, l_sum, l_xy, l_tot, l_z, l_half, l_other,
    e_own, e_sib, e_sum, e_xy, e_z,
    in_sem, zs, zr, xs, xr, ws, wr, fs, fr, ps, pr, qs, qr,
    gs, gr, gxs, gxr, ls, lr, lxs, lxr, lzs, lzr, us, ur, es, er, exs, exr, ezs, ezr,
):
    row = lax.axis_index("row")
    col = lax.axis_index("col")
    xy = lax.rem(row, 16)
    core = lax.rem(col, 2)
    z = (col // 2) * 4 + row // 16

    def dev(z_at, xy_at, core_at):
        return (lax.rem(z_at, 4) * 16 + xy_at, (z_at // 4) * 2 + core_at)

    def z_shift(k):
        far = 8 - (k + 1) // 2
        return jnp.where(lax.rem(k, 2) == 1, far, 16 - far)

    def z_peer(k):
        return lax.rem(z + z_shift(k), 16)

    def xy_peer(k):
        return lax.rem(xy + k, 16)

    sibling = dev(z, xy, 1 - core)

    def remote(src, dst, send, recv, where=sibling):
        return pltpu.make_async_remote_copy(
            src_ref=src, dst_ref=dst, send_sem=send, recv_sem=recv, device_id=where, device_id_type=MESH
        )

    def along_z(src, buf, send, recv):
        def copy(k):
            return remote(src, buf.at[z], send.at[k], recv.at[z], dev(z_peer(k), xy, core))

        def arrival(k):
            p = z_peer(k)
            return remote(src, buf.at[p], send.at[k], recv.at[p])

        return (
            lambda: loop(0, 15, lambda k: copy(k).start()),
            lambda: loop(0, 15, lambda k: arrival(k).wait_recv()),
            lambda: loop(0, 15, lambda k: copy(k).wait_send()),
        )

    def over_xy(src_of, buf, send, recv):
        def copy(k):
            p = xy_peer(k)
            return remote(src_of(p), buf.at[xy], send.at[k], recv.at[xy], dev(z, p, core))

        def arrival(k):
            p = xy_peer(k)
            return remote(src_of(p), buf.at[p], send.at[k], recv.at[p])

        return (
            lambda: loop(1, 16, lambda k: copy(k).start()),
            lambda: loop(1, 16, lambda k: arrival(k).wait_recv()),
            lambda: loop(1, 16, lambda k: copy(k).wait_send()),
        )

    barrier = pltpu.get_barrier_semaphore()

    def greet(where):
        pl.semaphore_signal(barrier, inc=1, device_id=where, device_id_type=MESH)

    loop(0, 15, lambda k: greet(dev(z_peer(k), xy, core)))
    loop(1, 16, lambda k: greet(dev(z, xy_peer(k), core)))
    greet(sibling)

    loads = [
        pltpu.make_async_copy(src, dst, in_sem.at[n])
        for n, (src, dst) in enumerate(
            (
                (feat_hbm, feat_in), (inv_hbm, inv_in), (piv_hbm, piv_in),
                (sol_hbm, sol_in), (res_hbm, res_in), (dir_hbm, dir_in),
            )
        )
    ]
    for load in loads:
        load.start()
    stage_a[...] = jnp.zeros((128, 128), f32)
    stage_b[...] = jnp.zeros((128, 128), f32)
    for load in loads:
        load.wait()

    lane = iota((64, 128), 1)
    line = iota((64, 128), 0)
    stage_a[0:32, 0:64] = dir_in[...]
    stage_a[64:128, 0:64] = feat_in[...].astype(f32)
    stage_b[0:32, 0:64] = res_in[...]
    stage_b[32:64, 0:64] = sol_in[...]
    turned = stage_a[...].T[0:64]
    others = stage_b[...].T[0:64]
    dir_t = jnp.where(lane < 32, turned, 0.0)
    res_t = jnp.where(lane < 32, others, 0.0)
    sol_t = jnp.where(lane < 32, pltpu.roll(others, 96, 1), 0.0)
    stage_a[0:1, 0:64] = inv_in[...]
    stage_a[0:1, 64:128] = jnp.zeros((1, 64), f32)
    inv_row = pltpu.roll(stage_a[0:8, :], 64, 1)[0:1]
    scaled = jnp.where(lane >= 64, (turned * inv_row).astype(bf16).astype(f32), 0.0)

    offset = (row * 8 + col) * 64
    hits = piv_in[...] == iota((64, 64), 0) + offset
    picked = jnp.max(jnp.where(hits, 1.0, 0.0), axis=1, keepdims=True)
    chosen = jnp.broadcast_to(jnp.sum(picked * scaled, axis=0, keepdims=True), (8, 128))
    row_form, col_form = forms(scaled, lane)
    for k in range(4):
        moved = pltpu.roll(chosen, (38 - 64 - 16 * k) % 128, 1)[0:1]
        row_form = row_form + jnp.where((line == k) & (lane >= 38) & (lane < 54), moved, 0.0)
    own_row = row_form.astype(bf16)
    own_col = (col_form + dir_t).astype(bf16)
    zbuf[0] = own_col
    xbuf[core, xy] = own_row

    pl.semaphore_wait(barrier, 31)

    def z_copy(k):
        return remote(zbuf.at[0], zbuf.at[k + 1], zs.at[k], zr.at[k], dev(z_peer(k), xy, core))

    x_start, x_arrive, x_left = over_xy(lambda p: xbuf.at[core, xy], xbuf.at[core], xs, xr)

    def w_copy(p):
        return remote(xbuf.at[core, p], xbuf.at[core, p], ws.at[p], wr.at[p])

    def w_arrival(p):
        return remote(xbuf.at[1 - core, p], xbuf.at[1 - core, p], ws.at[p], wr.at[p])

    loop(0, 15, lambda k: z_copy(k).start())
    x_start()
    w_copy(xy).start()

    def forward(k):
        p = xy_peer(k)
        remote(xbuf.at[core, p], xbuf.at[core, p], xs.at[k], xr.at[p]).wait_recv()
        w_copy(p).start()

    loop(1, 16, forward)
    loop(0, 16, lambda p: w_arrival(p).wait_recv())

    seen = (xbuf[0, :, 0:16, :].astype(f32) + xbuf[1, :, 0:16, :].astype(f32))[:, 0:8, :]
    at_lane = iota((16, 8, 128), 2)
    at_line = iota((16, 8, 128), 1)
    seen = jnp.where((at_lane >= 38) & (at_lane < 54), seen, 0.0).reshape(128, 128)
    found = jnp.zeros((16, 8, 128), f32)
    for k in range(4):
        found = found + jnp.where(at_line == k, pltpu.roll(seen, 64 + 16 * k - 38, 1).reshape(16, 8, 128), 0.0)
    q_z[z] = jnp.sum(found, axis=1).astype(bf16)
    q_start, q_arrive, q_left = along_z(q_z.at[z], q_z, qs, qr)
    q_start()

    lane_w = iota((256, 128), 1)

    def columns(group):
        held = zbuf[group * 4 : group * 4 + 4].reshape(256, 128)
        direction = jnp.where(lane_w < 32, held.astype(f32), 0.0)
        weights[0:256, :] = direction.astype(bf16)
        weights[256:512, :] = (pltpu.roll(direction, 32, 1) * -2.0).astype(bf16)
        return held

    def tile(rows, cols):
        half = lax.dot_general(rows, cols, NT, preferred_element_type=f32)
        value = jnp.exp(half)
        images = jnp.dot(value.astype(bf16), weights[0:256, :], preferred_element_type=f32)
        return images + jnp.dot((value * half).astype(bf16), weights[256:512, :], preferred_element_type=f32)

    def z_arrival(k):
        remote(zbuf.at[0], zbuf.at[k + 1], zs.at[k], zr.at[k]).wait_recv()

    for group in range(3):
        loop(max(group * 4 - 1, 0), group * 4 + 3, z_arrival)
        cols = columns(group)
        product = tile(xbuf[...].reshape(2048, 128), cols)
        if group == 0:
            acc[...] = product.reshape(2, 1024, 128)
        else:
            acc[...] += product.reshape(2, 1024, 128)
    loop(11, 15, z_arrival)
    cols = columns(3)

    def last(owner):
        total = acc[owner] + tile(xbuf[owner].reshape(1024, 128), cols)
        acc[owner] = total
        total = total.reshape(16, 64, 128)
        upper = total[:, 0:32].reshape(512, 128)
        lower = total[:, 32:64].reshape(512, 128)
        fold[owner] = (upper + pltpu.roll(lower, 64, 1)).reshape(16, 32, 128)

    last(1 - core)
    f_copy = remote(fold.at[1 - core], fold_sib, fs, fr)
    f_copy.start()
    last(core)

    q_arrive()
    lots = []
    for low in range(4):
        lot = q_z[low].astype(f32)
        for high in range(1, 4):
            lot = lot + q_z[high * 4 + low].astype(f32)
        lots.append(lot)
    pivot_row, pivot_col = forms(jnp.concatenate(lots, axis=0), lane)
    pivot_row = pivot_row.astype(bf16)
    pivot_col = pivot_col.astype(bf16)
    line_kernel = kernel_of(pivot_row, zbuf[...].reshape(1024, 128))
    gram_part = exact(line_kernel, line_kernel, NT)
    wide = jnp.concatenate([gram_part, jnp.zeros((64, 64), f32)], axis=1)
    g_own[...] = wide[0:32] + pltpu.roll(wide[32:64], 64, 1)
    g_copy = remote(g_own, g_sib, gs, gr)
    g_copy.start()

    f_copy.wait()
    part[...] = fold[core] + fold_sib[...]
    part_xy[xy] = part[xy]
    s_start, s_arrive, s_left = over_xy(lambda p: part.at[p], part_xy, ps, pr)
    s_start()

    own_kernel = kernel_of(pivot_row, own_col)
    own_kernel_t = kernel_of(own_row, pivot_col)
    pivot_self = kernel_of(pivot_row, pivot_col)
    plane_kernel = kernel_of(pivot_col, xbuf[...].reshape(2048, 128))
    proj = exact(plane_kernel, acc[...].reshape(2048, 128))
    proj = jnp.where(lane < 32, proj, 0.0) + exact(own_kernel, noise_var * dir_t + pltpu.roll(res_t, 32, 1))
    l_own[...] = proj[0:32] + pltpu.roll(proj[32:64], 64, 1)
    l_copy = remote(l_own, l_sib, ls, lr)
    l_copy.start()

    g_copy.wait()
    g_sum[...] = g_own[...] + g_sib[...]
    g_xy[xy] = g_sum[...]
    g_start, g_arrive, g_left = over_xy(lambda p: g_sum, g_xy, gxs, gxr)
    g_start()
    l_copy.wait()
    l_sum[...] = l_own[...] + l_sib[...]
    l_xy[xy] = l_sum[...]
    l_start, l_arrive, l_left = over_xy(lambda p: l_sum, l_xy, lxs, lxr)
    l_start()

    s_arrive()
    images = unfold(jnp.sum(part_xy[...], axis=0))
    image = jnp.where(lane < 32, images + noise_var * dir_t, 0.0)
    slope = jnp.where((lane >= 32) & (lane < 64), images, 0.0)
    sums = jnp.sum(
        dir_t * image
        + pltpu.roll(res_t * image, 32, 1)
        + pltpu.roll(image * image, 64, 1)
        + pltpu.roll(res_t * res_t, 96, 1),
        axis=0,
        keepdims=True,
    )
    e_own[...] = sums
    e_copy = remote(e_own, e_sib, es, er)
    e_copy.start()
    e_copy.wait()
    e_sum[...] = e_own[...] + e_sib[...]
    e_xy[xy] = e_sum[...]
    e_start, e_arrive, e_left = over_xy(lambda p: e_sum, e_xy, exs, exr)
    e_start()

    l_arrive()
    l_tot[...] = jnp.sum(l_xy[...], axis=0)
    l_z[z] = l_tot[pl.ds(pl.multiple_of(core * 16, 16), 16), :]
    lz_start, lz_arrive, lz_left = along_z(l_z.at[z], l_z, lzs, lzr)
    lz_start()

    g_arrive()
    gram = unfold(jnp.sum(g_xy[...], axis=0))
    own_self = jnp.concatenate([noise_var * pivot_self, jnp.zeros((64, 64), f32)], axis=1)
    work = jnp.where(lane < 64, gram + own_self, jnp.where(lane == line + 64, 1.0, 0.0))

    def eliminate(work, low, high):
        for k in range(low, high):
            head = work[k : k + 1, :]
            factor = work[:, k : k + 1] * (1.0 / head[:, k : k + 1])
            work = work - jnp.where(line > k, factor, 0.0) * head
        return work

    work = eliminate(work, 0, 24)
    e_arrive()
    e_z[z] = jnp.sum(e_xy[...], axis=0)
    ez_start, ez_arrive, ez_left = along_z(e_z.at[z], e_z, ezs, ezr)
    ez_start()
    work = eliminate(work, 24, 64)
    diagonal = jnp.sum(jnp.where(lane == line, work, 0.0), axis=1, keepdims=True)
    lower_inv = pltpu.roll(work, 64, 1)[:, 0:64] * lax.rsqrt(diagonal)
    gram_inv = exact(lower_inv.T, lower_inv)
    mapped = exact(own_kernel_t, gram_inv)

    loop(0, 15, lambda k: z_copy(k).wait_send())
    x_left()
    loop(0, 16, lambda p: w_copy(p).wait_send())
    q_left()
    s_left()
    g_left()
    l_left()
    e_left()

    lz_arrive()
    l_half[...] = jnp.sum(l_z[...], axis=0)
    u_copy = remote(l_half, l_other, us, ur)
    u_copy.start()
    lz_left()
    u_copy.wait()
    mine = l_half[...]
    other = l_other[...]
    projs = unfold(jnp.concatenate([jnp.where(core == 0, mine, other), jnp.where(core == 0, other, mine)], axis=0))
    solved = exact(gram_inv, projs)
    spread = exact(mapped, projs)

    def old(values):
        return pltpu.roll(values, 96, 1)

    proj_old = old(projs)
    solved_old = old(solved)
    spread_old = old(spread)
    removed_old = jnp.sum(proj_old * solved_old, axis=0, keepdims=True)

    ez_left()
    ez_arrive()
    curvature = jnp.sum(e_z[...], axis=0)
    cross = pltpu.roll(jnp.broadcast_to(curvature, (8, 128)), 96, 1)[0:1]
    square = pltpu.roll(jnp.broadcast_to(curvature, (8, 128)), 64, 1)[0:1]
    square_old = pltpu.roll(jnp.broadcast_to(curvature, (8, 128)), 32, 1)[0:1]
    norm_old = (square_old - removed_old) / noise_var
    step = norm_old / curvature
    residual_new = res_t - step * image
    proj_new = proj_old - step * projs
    solved_new = solved_old - step * solved
    square_new = square_old - 2.0 * step * cross + step * step * square
    norm_new = (square_new - jnp.sum(proj_new * solved_new, axis=0, keepdims=True)) / noise_var
    precond_new = (residual_new - (spread_old - step * spread)) / noise_var
    direction_new = precond_new + (norm_new / norm_old) * dir_t
    solution_new = sol_t + step * dir_t
    result[...] = jnp.where(
        lane < 32,
        solution_new,
        jnp.where(
            lane < 64,
            pltpu.roll(residual_new, 32, 1),
            jnp.where(lane < 96, pltpu.roll(direction_new, 64, 1), pltpu.roll(slope, 64, 1)),
        ),
    )


def turn_kernel(result, sol_out, res_out, dir_out, slope_out, stage):
    stage[0:64, :] = result[...]
    stage[64:128, :] = jnp.zeros((64, 128), f32)
    turned = stage[...].T
    sol_out[...] = turned[0:32, 0:64]
    res_out[...] = turned[32:64, 0:64]
    dir_out[...] = turned[64:96, 0:64]
    slope_out[...] = turned[96:128, 0:64]


def local(features, inv_scale, pivots, solution, residual, direction):
    vmem = pltpu.VMEM
    dma = pltpu.SemaphoreType.DMA
    one = dma(())
    many = dma((16,))
    fold32 = vmem((16, 32, 128), f32)
    flat32 = vmem((32, 128), f32)
    flat16 = vmem((16, 128), f32)
    flat1 = vmem((1, 128), f32)
    scratch = [
        vmem((64, 64), bf16), vmem((1, 64), f32), vmem((1, 64), jnp.int32),
        vmem((32, 64), f32), vmem((32, 64), f32), vmem((32, 64), f32),
        vmem((128, 128), f32), vmem((128, 128), f32),
        vmem((16, 64, 128), bf16), vmem((2, 16, 64, 128), bf16), vmem((512, 128), bf16), vmem((2, 1024, 128), f32),
        vmem((2, 16, 32, 128), f32), fold32, fold32, fold32,
        vmem((16, 16, 128), bf16),
        flat32, flat32, flat32, fold32,
        flat32, flat32, flat32, fold32, flat32, vmem((16, 16, 128), f32), flat16, flat16,
        flat1, flat1, flat1, vmem((16, 1, 128), f32), vmem((16, 1, 128), f32),
        dma((6,)), many, many, many, many, many, many, one, one, many, many, many, many,
        one, one, many, many, one, one, many, many, many, many, one, one, one, one, many, many, many, many,
    ]
    result = pl.pallas_call(
        step_kernel,
        name="cg_step",
        out_shape=jax.ShapeDtypeStruct((64, 128), f32),
        in_specs=[pl.BlockSpec(memory_space=pltpu.HBM)] * 6,
        out_specs=pl.BlockSpec(memory_space=vmem),
        scratch_shapes=scratch,
        compiler_params=pltpu.CompilerParams(
            collective_id=0, has_side_effects=True, vmem_limit_bytes=60 * 1024 * 1024
        ),
    )(features, inv_scale[None, :], pivots[None, :], solution, residual, direction)
    return pl.pallas_call(
        turn_kernel,
        name="turn",
        out_shape=(jax.ShapeDtypeStruct((32, 64), f32),) * 4,
        in_specs=[pl.BlockSpec(memory_space=vmem)],
        out_specs=(pl.BlockSpec(memory_space=vmem),) * 4,
        scratch_shapes=[vmem((128, 128), f32)],
    )(result)


def solution(mesh):
    split = P(None, ("row", "col"))
    return jax.shard_map(
        local,
        mesh=mesh,
        in_specs=(split, P(), P(), split, split, split),
        out_specs=(split,) * 4,
        check_vma=False,
    )
```

time: 77.2 us -> 64.4 us (0.83)
  Pallas kernels: 70.1 us -> 63.5 us
  local copies, waits for them, and re-layouts: 5.95 us -> 0 us
    pallas_call x1 -> x2, Pallas kernels: 70.1 us -> 63.5 us  [the longest x1 62.1 us: local(): pl.pallas_call(step_kernel, name='cg_step', out_shape=jax.ShapeDtypeStruc...]
    unnamed x16 -> x0, local copies, waits for them, and re-layouts: 5.95 us -> none
where the time goes in v2:
time: 64.4 us; the launch traced here: 64.2 us
  Pallas kernels  63.5 us (99%)
    pallas_call x1, Pallas kernels, local(): pl.pallas_call(step_kernel, name='cg_step', out_shape=jax.ShapeDtypeStruc...  62.1 us
    pallas_call x1, Pallas kernels, local(): pl.pallas_call(turn_kernel, name='turn', out_shape=(jax.ShapeDtypeStruct(...  1.47 us

profile of v2, /device:TPU:1, one launch (start us, length us, event | category | flops | bytes accessed | tf_op | source)
XLA Modules:
  0.0 64.2 jit_solution(6345847999948744468)
XLA Ops:
  0.6 62.1 %cg_step.1.result = f32[64,128]{1,0:T(8,128)} custom-call(bf16[64,64]{1,0:T(8,128)(2,1)} %feat_hbm.1, f32[1,64]{1,0:T(1,128)} %bitcast.2, s32[1,64]{1,0:T(1,128)} %bitcast.3, f32[32,64]{1,0:T(8,128)} %sol_hbm.1, f32[32,64]{1,0:T(8,128)} %res_hbm.1, f32[32,64]{1,0:T(8,128)} %dir_hbm.1), custom_call_target="tpu_custom_call" | custom-call | tf_op jit(solution)/shard_map/cg_step/pallas_call | solution.py:441
  62.7 1.5 %turn.1 = (f32[32,64]{1,0:T(8,128)}, f32[32,64]{1,0:T(8,128)}, f32[32,64]{1,0:T(8,128)}, f32[32,64]{1,0:T(8,128)}) custom-call(f32[64,128]{1,0:T(8,128)} %cg_step.1.result), custom_call_target="tpu_custom_call" | custom-call | tf_op jit(solution)/shard_map/turn/pallas_call | solution.py:452

commit v3 on v2

--- a/solution.py
+++ b/solution.py
@@ -60,13 +60,13 @@
     result,
     feat_in, inv_in, piv_in, sol_in, res_in, dir_in,
     stage_a, stage_b,
-    zbuf, xbuf, weights, acc,
-    fold, fold_sib, part, part_xy,
-    q_z,
+    zbuf, zsib, xbuf, weights, acc,
+    part, part_xy,
+    q_z, q_own, q_sib, q_xy,
     g_own, g_sib, g_sum, g_xy,
     l_own, l_sib, l_sum, l_xy, l_tot, l_z, l_half, l_other,
     e_own, e_sib, e_sum, e_xy, e_z,
-    in_sem, zs, zr, xs, xr, ws, wr, fs, fr, ps, pr, qs, qr,
+    in_sem, zs, zr, xs, xr, ws, wr, ps, pr, qs, qr, qcs, qcr, qxs, qxr,
     gs, gr, gxs, gxr, ls, lr, lxs, lxr, lzs, lzr, us, ur, es, er, exs, exr, ezs, ezr,
 ):
     row = lax.axis_index("row")
@@ -168,101 +168,91 @@
     offset = (row * 8 + col) * 64
     hits = piv_in[...] == iota((64, 64), 0) + offset
     picked = jnp.max(jnp.where(hits, 1.0, 0.0), axis=1, keepdims=True)
-    chosen = jnp.broadcast_to(jnp.sum(picked * scaled, axis=0, keepdims=True), (8, 128))
+    q_z[z] = jnp.sum(picked * scaled, axis=0, keepdims=True)
     row_form, col_form = forms(scaled, lane)
-    for k in range(4):
-        moved = pltpu.roll(chosen, (38 - 64 - 16 * k) % 128, 1)[0:1]
-        row_form = row_form + jnp.where((line == k) & (lane >= 38) & (lane < 54), moved, 0.0)
     own_row = row_form.astype(bf16)
     own_col = (col_form + dir_t).astype(bf16)
     zbuf[0] = own_col
-    xbuf[core, xy] = own_row
+    xbuf[xy] = own_row
 
     pl.semaphore_wait(barrier, 31)
+
+    q_start, q_arrive, q_left = along_z(q_z.at[z], q_z, qs, qr)
 
     def z_copy(k):
         return remote(zbuf.at[0], zbuf.at[k + 1], zs.at[k], zr.at[k], dev(z_peer(k), xy, core))
 
-    x_start, x_arrive, x_left = over_xy(lambda p: xbuf.at[core, xy], xbuf.at[core], xs, xr)
-
-    def w_copy(p):
-        return remote(xbuf.at[core, p], xbuf.at[core, p], ws.at[p], wr.at[p])
-
-    def w_arrival(p):
-        return remote(xbuf.at[1 - core, p], xbuf.at[1 - core, p], ws.at[p], wr.at[p])
-
+    def z_arrival(k):
+        remote(zbuf.at[0], zbuf.at[k + 1], zs.at[k], zr.at[k]).wait_recv()
+
+    def w_copy(slot):
+        return remote(zbuf.at[slot], zsib.at[slot], ws.at[slot], wr.at[slot])
+
+    x_start, x_arrive, x_left = over_xy(lambda p: xbuf.at[xy], xbuf, xs, xr)
+    q_start()
     loop(0, 15, lambda k: z_copy(k).start())
     x_start()
-    w_copy(xy).start()
-
-    def forward(k):
-        p = xy_peer(k)
-        remote(xbuf.at[core, p], xbuf.at[core, p], xs.at[k], xr.at[p]).wait_recv()
-        w_copy(p).start()
-
-    loop(1, 16, forward)
-    loop(0, 16, lambda p: w_arrival(p).wait_recv())
-
-    seen = (xbuf[0, :, 0:16, :].astype(f32) + xbuf[1, :, 0:16, :].astype(f32))[:, 0:8, :]
-    at_lane = iota((16, 8, 128), 2)
-    at_line = iota((16, 8, 128), 1)
-    seen = jnp.where((at_lane >= 38) & (at_lane < 54), seen, 0.0).reshape(128, 128)
-    found = jnp.zeros((16, 8, 128), f32)
-    for k in range(4):
-        found = found + jnp.where(at_line == k, pltpu.roll(seen, 64 + 16 * k - 38, 1).reshape(16, 8, 128), 0.0)
-    q_z[z] = jnp.sum(found, axis=1).astype(bf16)
-    q_start, q_arrive, q_left = along_z(q_z.at[z], q_z, qs, qr)
-    q_start()
-
-    lane_w = iota((256, 128), 1)
-
-    def columns(group):
-        held = zbuf[group * 4 : group * 4 + 4].reshape(256, 128)
-        direction = jnp.where(lane_w < 32, held.astype(f32), 0.0)
-        weights[0:256, :] = direction.astype(bf16)
-        weights[256:512, :] = (pltpu.roll(direction, 32, 1) * -2.0).astype(bf16)
-        return held
-
-    def tile(rows, cols):
-        half = lax.dot_general(rows, cols, NT, preferred_element_type=f32)
+    w_copy(0).start()
+
+    def tile(cols):
+        count = cols.shape[0]
+        direction = jnp.where(iota((count, 128), 1) < 32, cols.astype(f32), 0.0)
+        weights[0:count, :] = direction.astype(bf16)
+        weights[count : 2 * count, :] = (pltpu.roll(direction, 32, 1) * -2.0).astype(bf16)
+        half = lax.dot_general(xbuf[...].reshape(1024, 128), cols, NT, preferred_element_type=f32)
         value = jnp.exp(half)
-        images = jnp.dot(value.astype(bf16), weights[0:256, :], preferred_element_type=f32)
-        return images + jnp.dot((value * half).astype(bf16), weights[256:512, :], preferred_element_type=f32)
-
-    def z_arrival(k):
-        remote(zbuf.at[0], zbuf.at[k + 1], zs.at[k], zr.at[k]).wait_recv()
-
-    for group in range(3):
-        loop(max(group * 4 - 1, 0), group * 4 + 3, z_arrival)
-        cols = columns(group)
-        product = tile(xbuf[...].reshape(2048, 128), cols)
-        if group == 0:
-            acc[...] = product.reshape(2, 1024, 128)
-        else:
-            acc[...] += product.reshape(2, 1024, 128)
-    loop(11, 15, z_arrival)
-    cols = columns(3)
-
-    def last(owner):
-        total = acc[owner] + tile(xbuf[owner].reshape(1024, 128), cols)
-        acc[owner] = total
-        total = total.reshape(16, 64, 128)
-        upper = total[:, 0:32].reshape(512, 128)
-        lower = total[:, 32:64].reshape(512, 128)
-        fold[owner] = (upper + pltpu.roll(lower, 64, 1)).reshape(16, 32, 128)
-
-    last(1 - core)
-    f_copy = remote(fold.at[1 - core], fold_sib, fs, fr)
-    f_copy.start()
-    last(core)
+        images = jnp.dot(value.astype(bf16), weights[0:count, :], preferred_element_type=f32)
+        return images + jnp.dot((value * half).astype(bf16), weights[count : 2 * count, :], preferred_element_type=f32)
+
+    def receive(k):
+        z_arrival(k)
+        w_copy(k + 1).start()
+
+    def lines(group):
+        loop(max(group * 4 - 1, 0), group * 4 + 3, receive)
+        return zbuf[group * 4 : group * 4 + 4].reshape(256, 128)
+
+    def sibling_lines(group):
+        loop(group * 4, group * 4 + 4, lambda slot: w_copy(slot).wait_recv())
+        return zsib[group * 4 : group * 4 + 4].reshape(256, 128)
+
+    x_arrive()
+    cols = lines(0)
+    acc[...] = tile(cols)
 
     q_arrive()
-    lots = []
+    line8 = iota((8, 128), 0)
+    found = jnp.zeros((8, 128), f32)
     for low in range(4):
-        lot = q_z[low].astype(f32)
-        for high in range(1, 4):
-            lot = lot + q_z[high * 4 + low].astype(f32)
-        lots.append(lot)
+        lot = q_z[low] + q_z[4 + low] + q_z[8 + low] + q_z[12 + low]
+        found = found + jnp.where(line8 == lax.rem(xy, 2) * 4 + low, lot, 0.0)
+    q_own[...] = found
+    qc_copy = remote(q_own, q_sib, qcs, qcr)
+    qc_copy.start()
+
+    cols = lines(1)
+    acc[...] += tile(jnp.concatenate([cols, sibling_lines(0)], axis=0))
+    qc_copy.wait()
+    q_xy[xy] = q_own[...] + q_sib[...]
+    qx_start, qx_arrive, qx_left = over_xy(lambda p: q_xy.at[xy], q_xy, qxs, qxr)
+    qx_start()
+    cols = lines(2)
+    acc[...] += tile(jnp.concatenate([cols, sibling_lines(1)], axis=0))
+    cols = lines(3)
+    acc[...] += tile(jnp.concatenate([cols, sibling_lines(2)], axis=0))
+    total = acc[...] + tile(sibling_lines(3))
+    acc[...] = total
+
+    total = total.reshape(16, 64, 128)
+    upper = total[:, 0:32].reshape(512, 128)
+    lower = total[:, 32:64].reshape(512, 128)
+    part[...] = (upper + pltpu.roll(lower, 64, 1)).reshape(16, 32, 128)
+    part_xy[xy] = part[xy]
+    s_start, s_arrive, s_left = over_xy(lambda p: part.at[p], part_xy, ps, pr)
+    s_start()
+
+    qx_arrive()
+    lots = [q_xy[2 * pair] + q_xy[2 * pair + 1] for pair in range(8)]
     pivot_row, pivot_col = forms(jnp.concatenate(lots, axis=0), lane)
     pivot_row = pivot_row.astype(bf16)
     pivot_col = pivot_col.astype(bf16)
@@ -273,17 +263,11 @@
     g_copy = remote(g_own, g_sib, gs, gr)
     g_copy.start()
 
-    f_copy.wait()
-    part[...] = fold[core] + fold_sib[...]
-    part_xy[xy] = part[xy]
-    s_start, s_arrive, s_left = over_xy(lambda p: part.at[p], part_xy, ps, pr)
-    s_start()
-
     own_kernel = kernel_of(pivot_row, own_col)
     own_kernel_t = kernel_of(own_row, pivot_col)
     pivot_self = kernel_of(pivot_row, pivot_col)
-    plane_kernel = kernel_of(pivot_col, xbuf[...].reshape(2048, 128))
-    proj = exact(plane_kernel, acc[...].reshape(2048, 128))
+    plane_kernel = kernel_of(pivot_col, xbuf[...].reshape(1024, 128))
+    proj = exact(plane_kernel, acc[...])
     proj = jnp.where(lane < 32, proj, 0.0) + exact(own_kernel, noise_var * dir_t + pltpu.roll(res_t, 32, 1))
     l_own[...] = proj[0:32] + pltpu.roll(proj[32:64], 64, 1)
     l_copy = remote(l_own, l_sib, ls, lr)
@@ -354,6 +338,7 @@
     x_left()
     loop(0, 16, lambda p: w_copy(p).wait_send())
     q_left()
+    qx_left()
     s_left()
     g_left()
     l_left()
@@ -429,13 +414,14 @@
         vmem((64, 64), bf16), vmem((1, 64), f32), vmem((1, 64), jnp.int32),
         vmem((32, 64), f32), vmem((32, 64), f32), vmem((32, 64), f32),
         vmem((128, 128), f32), vmem((128, 128), f32),
-        vmem((16, 64, 128), bf16), vmem((2, 16, 64, 128), bf16), vmem((512, 128), bf16), vmem((2, 1024, 128), f32),
-        vmem((2, 16, 32, 128), f32), fold32, fold32, fold32,
-        vmem((16, 16, 128), bf16),
+        vmem((16, 64, 128), bf16), vmem((16, 64, 128), bf16), vmem((16, 64, 128), bf16),
+        vmem((1024, 128), bf16), vmem((1024, 128), f32),
+        fold32, fold32,
+        vmem((16, 1, 128), f32), vmem((8, 128), f32), vmem((8, 128), f32), vmem((16, 8, 128), f32),
         flat32, flat32, flat32, fold32,
         flat32, flat32, flat32, fold32, flat32, vmem((16, 16, 128), f32), flat16, flat16,
         flat1, flat1, flat1, vmem((16, 1, 128), f32), vmem((16, 1, 128), f32),
-        dma((6,)), many, many, many, many, many, many, one, one, many, many, many, many,
+        dma((6,)), many, many, many, many, many, many, many, many, many, many, one, one, many, many,
         one, one, many, many, one, one, many, many, many, many, one, one, one, one, many, many, many, many,
     ]
     result = pl.pallas_call(

time: 64.4 us -> 64.8 us (level)
  no operation moved by 1% of the time
where the time goes in v3:
time: 64.8 us; the launch traced here: 64.5 us
  Pallas kernels  63.9 us (99%)
    pallas_call x1, Pallas kernels, local(): pl.pallas_call(step_kernel, name='cg_step', out_shape=jax.ShapeDtypeStruc...  62.4 us
    pallas_call x1, Pallas kernels, local(): pl.pallas_call(turn_kernel, name='turn', out_shape=(jax.ShapeDtypeStruct(...  1.47 us

profile of v3, /device:TPU:1, one launch (start us, length us, event | category | flops | bytes accessed | tf_op | source)
XLA Modules:
  0.0 64.5 jit_solution(559448265963740639)
XLA Ops:
  0.6 62.4 %cg_step.1.result = f32[64,128]{1,0:T(8,128)} custom-call(bf16[64,64]{1,0:T(8,128)(2,1)} %feat_hbm.1, f32[1,64]{1,0:T(1,128)} %bitcast.2, s32[1,64]{1,0:T(1,128)} %bitcast.3, f32[32,64]{1,0:T(8,128)} %sol_hbm.1, f32[32,64]{1,0:T(8,128)} %res_hbm.1, f32[32,64]{1,0:T(8,128)} %dir_hbm.1), custom_call_target="tpu_custom_call" | custom-call | tf_op jit(solution)/shard_map/cg_step/pallas_call | solution.py:427
  63.0 1.5 %turn.1 = (f32[32,64]{1,0:T(8,128)}, f32[32,64]{1,0:T(8,128)}, f32[32,64]{1,0:T(8,128)}, f32[32,64]{1,0:T(8,128)}) custom-call(f32[64,128]{1,0:T(8,128)} %cg_step.1.result), custom_call_target="tpu_custom_call" | custom-call | tf_op jit(solution)/shard_map/turn/pallas_call | solution.py:438

commit v4 on v3

--- a/solution.py
+++ b/solution.py
@@ -51,6 +51,25 @@
     return row_form, col_form
 
 
+def unfold_block(blocks):
+    count = blocks.shape[0]
+    wide = blocks.astype(f32)
+    lane = iota((count * 64, 128), 1)
+    near = wide[:, 0:32]
+    far = pltpu.roll(near.reshape(count * 32, 128), 64, 1).reshape(count, 32, 128)
+    scaled = jnp.concatenate([near, far], axis=1).reshape(count * 64, 128)
+    column = forms(jnp.where(lane >= 64, scaled, 0.0), lane)[1].astype(bf16)
+    packed = wide[:, 32:48].reshape(count * 16, 128)
+
+    def at(first):
+        turned = [pltpu.roll(packed, (first - 32 * q) % 128, 1).reshape(count, 16, 128) for q in range(4)]
+        return jnp.concatenate(turned, axis=1).reshape(count * 64, 128)
+
+    plain = jnp.where(lane < 32, at(0), 0.0).astype(bf16)
+    slope = jnp.where((lane >= 32) & (lane < 64), -2.0 * at(32), 0.0).astype(bf16)
+    return column, plain, slope
+
+
 def unfold(packed):
     return jnp.concatenate([packed, pltpu.roll(packed, 64, 1)], axis=0)
 
@@ -60,7 +79,7 @@
     result,
     feat_in, inv_in, piv_in, sol_in, res_in, dir_in,
     stage_a, stage_b,
-    zbuf, zsib, xbuf, weights, acc,
+    zbuf, zsib, xbuf, colm, acc,
     part, part_xy,
     q_z, q_own, q_sib, q_xy,
     g_own, g_sib, g_sum, g_xy,
@@ -171,8 +190,11 @@
     q_z[z] = jnp.sum(picked * scaled, axis=0, keepdims=True)
     row_form, col_form = forms(scaled, lane)
     own_row = row_form.astype(bf16)
-    own_col = (col_form + dir_t).astype(bf16)
-    zbuf[0] = own_col
+    own_col = col_form.astype(bf16)
+    zbuf[0, 0:32, :] = (scaled[0:32] + pltpu.roll(scaled[32:64], 64, 1)).astype(bf16)
+    zbuf[0, 32:48, :] = sum(
+        (pltpu.roll(dir_t[16 * q : 16 * q + 16], 32 * q, 1) for q in range(1, 4)), dir_t[0:16]
+    ).astype(bf16)
     xbuf[xy] = own_row
 
     pl.semaphore_wait(barrier, 31)
@@ -194,15 +216,14 @@
     x_start()
     w_copy(0).start()
 
-    def tile(cols):
-        count = cols.shape[0]
-        direction = jnp.where(iota((count, 128), 1) < 32, cols.astype(f32), 0.0)
-        weights[0:count, :] = direction.astype(bf16)
-        weights[count : 2 * count, :] = (pltpu.roll(direction, 32, 1) * -2.0).astype(bf16)
+    def tile(blocks, keep=None):
+        cols, plain, slope = unfold_block(blocks)
+        if keep is not None:
+            colm[keep * 256 : keep * 256 + 256, :] = cols[0:256]
         half = lax.dot_general(xbuf[...].reshape(1024, 128), cols, NT, preferred_element_type=f32)
         value = jnp.exp(half)
-        images = jnp.dot(value.astype(bf16), weights[0:count, :], preferred_element_type=f32)
-        return images + jnp.dot((value * half).astype(bf16), weights[count : 2 * count, :], preferred_element_type=f32)
+        images = jnp.dot(value.astype(bf16), plain, preferred_element_type=f32)
+        return images + jnp.dot((value * half).astype(bf16), slope, preferred_element_type=f32)
 
     def receive(k):
         z_arrival(k)
@@ -210,15 +231,14 @@
 
     def lines(group):
         loop(max(group * 4 - 1, 0), group * 4 + 3, receive)
-        return zbuf[group * 4 : group * 4 + 4].reshape(256, 128)
+        return zbuf[group * 4 : group * 4 + 4]
 
     def sibling_lines(group):
         loop(group * 4, group * 4 + 4, lambda slot: w_copy(slot).wait_recv())
-        return zsib[group * 4 : group * 4 + 4].reshape(256, 128)
+        return zsib[group * 4 : group * 4 + 4]
 
     x_arrive()
-    cols = lines(0)
-    acc[...] = tile(cols)
+    acc[...] = tile(lines(0), 0)
 
     q_arrive()
     line8 = iota((8, 128), 0)
@@ -230,16 +250,16 @@
     qc_copy = remote(q_own, q_sib, qcs, qcr)
     qc_copy.start()
 
-    cols = lines(1)
-    acc[...] += tile(jnp.concatenate([cols, sibling_lines(0)], axis=0))
+    blocks = lines(1)
+    acc[...] += tile(jnp.concatenate([blocks, sibling_lines(0)], axis=0), 1)
     qc_copy.wait()
     q_xy[xy] = q_own[...] + q_sib[...]
     qx_start, qx_arrive, qx_left = over_xy(lambda p: q_xy.at[xy], q_xy, qxs, qxr)
     qx_start()
-    cols = lines(2)
-    acc[...] += tile(jnp.concatenate([cols, sibling_lines(1)], axis=0))
-    cols = lines(3)
-    acc[...] += tile(jnp.concatenate([cols, sibling_lines(2)], axis=0))
+    blocks = lines(2)
+    acc[...] += tile(jnp.concatenate([blocks, sibling_lines(1)], axis=0), 2)
+    blocks = lines(3)
+    acc[...] += tile(jnp.concatenate([blocks, sibling_lines(2)], axis=0), 3)
     total = acc[...] + tile(sibling_lines(3))
     acc[...] = total
 
@@ -256,16 +276,7 @@
     pivot_row, pivot_col = forms(jnp.concatenate(lots, axis=0), lane)
     pivot_row = pivot_row.astype(bf16)
     pivot_col = pivot_col.astype(bf16)
-    line_kernel = kernel_of(pivot_row, zbuf[...].reshape(1024, 128))
-    gram_part = exact(line_kernel, line_kernel, NT)
-    wide = jnp.concatenate([gram_part, jnp.zeros((64, 64), f32)], axis=1)
-    g_own[...] = wide[0:32] + pltpu.roll(wide[32:64], 64, 1)
-    g_copy = remote(g_own, g_sib, gs, gr)
-    g_copy.start()
-
     own_kernel = kernel_of(pivot_row, own_col)
-    own_kernel_t = kernel_of(own_row, pivot_col)
-    pivot_self = kernel_of(pivot_row, pivot_col)
     plane_kernel = kernel_of(pivot_col, xbuf[...].reshape(1024, 128))
     proj = exact(plane_kernel, acc[...])
     proj = jnp.where(lane < 32, proj, 0.0) + exact(own_kernel, noise_var * dir_t + pltpu.roll(res_t, 32, 1))
@@ -273,16 +284,24 @@
     l_copy = remote(l_own, l_sib, ls, lr)
     l_copy.start()
 
+    line_kernel = kernel_of(pivot_row, colm[...])
+    gram_part = exact(line_kernel, line_kernel, NT)
+    wide = jnp.concatenate([gram_part, jnp.zeros((64, 64), f32)], axis=1)
+    g_own[...] = wide[0:32] + pltpu.roll(wide[32:64], 64, 1)
+    g_copy = remote(g_own, g_sib, gs, gr)
+    g_copy.start()
+    l_copy.wait()
+    l_sum[...] = l_own[...] + l_sib[...]
+    l_xy[xy] = l_sum[...]
+    l_start, l_arrive, l_left = over_xy(lambda p: l_sum, l_xy, lxs, lxr)
+    l_start()
+    own_kernel_t = kernel_of(own_row, pivot_col)
+    pivot_self = kernel_of(pivot_row, pivot_col)
     g_copy.wait()
     g_sum[...] = g_own[...] + g_sib[...]
     g_xy[xy] = g_sum[...]
     g_start, g_arrive, g_left = over_xy(lambda p: g_sum, g_xy, gxs, gxr)
     g_start()
-    l_copy.wait()
-    l_sum[...] = l_own[...] + l_sib[...]
-    l_xy[xy] = l_sum[...]
-    l_start, l_arrive, l_left = over_xy(lambda p: l_sum, l_xy, lxs, lxr)
-    l_start()
 
     s_arrive()
     images = unfold(jnp.sum(part_xy[...], axis=0))
@@ -414,7 +433,7 @@
         vmem((64, 64), bf16), vmem((1, 64), f32), vmem((1, 64), jnp.int32),
         vmem((32, 64), f32), vmem((32, 64), f32), vmem((32, 64), f32),
         vmem((128, 128), f32), vmem((128, 128), f32),
-        vmem((16, 64, 128), bf16), vmem((16, 64, 128), bf16), vmem((16, 64, 128), bf16),
+        vmem((16, 48, 128), bf16), vmem((16, 48, 128), bf16), vmem((16, 64, 128), bf16),
         vmem((1024, 128), bf16), vmem((1024, 128), f32),
         fold32, fold32,
         vmem((16, 1, 128), f32), vmem((8, 128), f32), vmem((8, 128), f32), vmem((16, 8, 128), f32),

time: 64.8 us -> 61.2 us (0.944)
  Pallas kernels: 63.9 us -> 60.3 us
    pallas_call x1, Pallas kernels: 62.4 us -> 58.8 us  [local(): pl.pallas_call(step_kernel, name='cg_step', out_shape=jax.ShapeDtypeStruc...]
where the time goes in v4:
time: 61.2 us; the launch traced here: 61 us
  Pallas kernels  60.3 us (99%)
  between operations  0.64 us (1%)
    pallas_call x1, Pallas kernels, local(): pl.pallas_call(step_kernel, name='cg_step', out_shape=jax.ShapeDtypeStruc...  58.8 us
    pallas_call x1, Pallas kernels, local(): pl.pallas_call(turn_kernel, name='turn', out_shape=(jax.ShapeDtypeStruct(...  1.47 us

profile of v4, /device:TPU:1, one launch (start us, length us, event | category | flops | bytes accessed | tf_op | source)
XLA Modules:
  0.0 61.0 jit_solution(1107611294111507134)
XLA Ops:
  0.6 58.8 %cg_step.1.result = f32[64,128]{1,0:T(8,128)} custom-call(bf16[64,64]{1,0:T(8,128)(2,1)} %feat_hbm.1, f32[1,64]{1,0:T(1,128)} %bitcast.2, s32[1,64]{1,0:T(1,128)} %bitcast.3, f32[32,64]{1,0:T(8,128)} %sol_hbm.1, f32[32,64]{1,0:T(8,128)} %res_hbm.1, f32[32,64]{1,0:T(8,128)} %dir_hbm.1), custom_call_target="tpu_custom_call" | custom-call | tf_op jit(solution)/shard_map/cg_step/pallas_call | solution.py:446
  59.5 1.5 %turn.1 = (f32[32,64]{1,0:T(8,128)}, f32[32,64]{1,0:T(8,128)}, f32[32,64]{1,0:T(8,128)}, f32[32,64]{1,0:T(8,128)}) custom-call(f32[64,128]{1,0:T(8,128)} %cg_step.1.result), custom_call_target="tpu_custom_call" | custom-call | tf_op jit(solution)/shard_map/turn/pallas_call | solution.py:457

commit v5 on v4

--- a/solution.py
+++ b/solution.py
@@ -82,11 +82,11 @@
     zbuf, zsib, xbuf, colm, acc,
     part, part_xy,
     q_z, q_own, q_sib, q_xy,
-    g_own, g_sib, g_sum, g_xy,
-    l_own, l_sib, l_sum, l_xy, l_tot, l_z, l_half, l_other,
+    g_own, g_sib, g_sum, g_xy, g_half, g_other,
+    l_own, l_sib, l_sum, l_xy, l_z, l_half, l_other,
     e_own, e_sib, e_sum, e_xy, e_z,
     in_sem, zs, zr, xs, xr, ws, wr, ps, pr, qs, qr, qcs, qcr, qxs, qxr,
-    gs, gr, gxs, gxr, ls, lr, lxs, lxr, lzs, lzr, us, ur, es, er, exs, exr, ezs, ezr,
+    gs, gr, gxs, gxr, vs, vr, ls, lr, lxs, lxr, lzs, lzr, us, ur, es, er, exs, exr, ezs, ezr,
 ):
     row = lax.axis_index("row")
     col = lax.axis_index("col")
@@ -108,11 +108,18 @@
         return lax.rem(xy + k, 16)
 
     sibling = dev(z, xy, 1 - core)
+    kept = pl.ds(pl.multiple_of(core * 16, 16), 16)
+    given = pl.ds(pl.multiple_of((1 - core) * 16, 16), 16)
 
     def remote(src, dst, send, recv, where=sibling):
         return pltpu.make_async_remote_copy(
             src_ref=src, dst_ref=dst, send_sem=send, recv_sem=recv, device_id=where, device_id_type=MESH
         )
+
+    def halves(mine, other):
+        first = jnp.where(core == 0, mine, other)
+        second = jnp.where(core == 0, other, mine)
+        return unfold(jnp.concatenate([first, second], axis=0))
 
     def along_z(src, buf, send, recv):
         def copy(k):
@@ -201,44 +208,56 @@
 
     q_start, q_arrive, q_left = along_z(q_z.at[z], q_z, qs, qr)
 
+    def z_near(k):
+        far = 4 - k // 2
+        return dev(lax.rem(z + jnp.where(lax.rem(k, 2) == 0, far, 16 - far), 16), xy, core)
+
     def z_copy(k):
-        return remote(zbuf.at[0], zbuf.at[k + 1], zs.at[k], zr.at[k], dev(z_peer(k), xy, core))
-
-    def z_arrival(k):
-        remote(zbuf.at[0], zbuf.at[k + 1], zs.at[k], zr.at[k]).wait_recv()
+        return remote(zbuf.at[0], zbuf.at[k + 1], zs.at[k], zr.at[k], z_near(k))
+
+    def relay_up(k):
+        return remote(zbuf.at[1], zbuf.at[k + 9], zs.at[k + 8], zr.at[k + 8], dev(lax.rem(z + 4 - k, 16), xy, core))
+
+    def relay_down(k):
+        return remote(zbuf.at[2], zbuf.at[k + 13], zs.at[k + 12], zr.at[k + 12], dev(lax.rem(z + 13 + k, 16), xy, core))
+
+    def z_arrival(slot):
+        remote(zbuf.at[0], zbuf.at[slot], zs.at[slot - 1], zr.at[slot - 1]).wait_recv()
 
     def w_copy(slot):
         return remote(zbuf.at[slot], zsib.at[slot], ws.at[slot], wr.at[slot])
 
+    def receive(slot):
+        z_arrival(slot)
+        w_copy(slot).start()
+
     x_start, x_arrive, x_left = over_xy(lambda p: xbuf.at[xy], xbuf, xs, xr)
+    loop(0, 8, lambda k: z_copy(k).start())
     q_start()
-    loop(0, 15, lambda k: z_copy(k).start())
     x_start()
     w_copy(0).start()
 
     def tile(blocks, keep=None):
         cols, plain, slope = unfold_block(blocks)
         if keep is not None:
-            colm[keep * 256 : keep * 256 + 256, :] = cols[0:256]
+            colm[keep * 512 : keep * 512 + 512, :] = cols
         half = lax.dot_general(xbuf[...].reshape(1024, 128), cols, NT, preferred_element_type=f32)
         value = jnp.exp(half)
         images = jnp.dot(value.astype(bf16), plain, preferred_element_type=f32)
         return images + jnp.dot((value * half).astype(bf16), slope, preferred_element_type=f32)
 
-    def receive(k):
-        z_arrival(k)
-        w_copy(k + 1).start()
-
-    def lines(group):
-        loop(max(group * 4 - 1, 0), group * 4 + 3, receive)
-        return zbuf[group * 4 : group * 4 + 4]
-
     def sibling_lines(group):
-        loop(group * 4, group * 4 + 4, lambda slot: w_copy(slot).wait_recv())
-        return zsib[group * 4 : group * 4 + 4]
-
+        loop(group * 8, group * 8 + 8, lambda slot: w_copy(slot).wait_recv())
+        return zsib[group * 8 : group * 8 + 8]
+
+    z_arrival(1)
+    loop(0, 4, lambda k: relay_up(k).start())
+    z_arrival(2)
+    loop(0, 3, lambda k: relay_down(k).start())
+    loop(1, 3, lambda slot: w_copy(slot).start())
+    loop(3, 9, receive)
     x_arrive()
-    acc[...] = tile(lines(0), 0)
+    acc[...] = tile(zbuf[0:8], 0)
 
     q_arrive()
     line8 = iota((8, 128), 0)
@@ -250,17 +269,14 @@
     qc_copy = remote(q_own, q_sib, qcs, qcr)
     qc_copy.start()
 
-    blocks = lines(1)
-    acc[...] += tile(jnp.concatenate([blocks, sibling_lines(0)], axis=0), 1)
+    acc[...] += tile(sibling_lines(0))
     qc_copy.wait()
     q_xy[xy] = q_own[...] + q_sib[...]
     qx_start, qx_arrive, qx_left = over_xy(lambda p: q_xy.at[xy], q_xy, qxs, qxr)
     qx_start()
-    blocks = lines(2)
-    acc[...] += tile(jnp.concatenate([blocks, sibling_lines(1)], axis=0), 2)
-    blocks = lines(3)
-    acc[...] += tile(jnp.concatenate([blocks, sibling_lines(2)], axis=0), 3)
-    total = acc[...] + tile(sibling_lines(3))
+    loop(9, 16, receive)
+    acc[...] += tile(zbuf[8:16], 1)
+    total = acc[...] + tile(sibling_lines(1))
     acc[...] = total
 
     total = total.reshape(16, 64, 128)
@@ -281,24 +297,24 @@
     proj = exact(plane_kernel, acc[...])
     proj = jnp.where(lane < 32, proj, 0.0) + exact(own_kernel, noise_var * dir_t + pltpu.roll(res_t, 32, 1))
     l_own[...] = proj[0:32] + pltpu.roll(proj[32:64], 64, 1)
-    l_copy = remote(l_own, l_sib, ls, lr)
+    l_copy = remote(l_own.at[given], l_sib, ls, lr)
     l_copy.start()
 
     line_kernel = kernel_of(pivot_row, colm[...])
     gram_part = exact(line_kernel, line_kernel, NT)
     wide = jnp.concatenate([gram_part, jnp.zeros((64, 64), f32)], axis=1)
     g_own[...] = wide[0:32] + pltpu.roll(wide[32:64], 64, 1)
-    g_copy = remote(g_own, g_sib, gs, gr)
+    g_copy = remote(g_own.at[given], g_sib, gs, gr)
     g_copy.start()
     l_copy.wait()
-    l_sum[...] = l_own[...] + l_sib[...]
+    l_sum[...] = l_own[kept, :] + l_sib[...]
     l_xy[xy] = l_sum[...]
     l_start, l_arrive, l_left = over_xy(lambda p: l_sum, l_xy, lxs, lxr)
     l_start()
     own_kernel_t = kernel_of(own_row, pivot_col)
     pivot_self = kernel_of(pivot_row, pivot_col)
     g_copy.wait()
-    g_sum[...] = g_own[...] + g_sib[...]
+    g_sum[...] = g_own[kept, :] + g_sib[...]
     g_xy[xy] = g_sum[...]
     g_start, g_arrive, g_left = over_xy(lambda p: g_sum, g_xy, gxs, gxr)
     g_start()
@@ -325,13 +341,20 @@
     e_start()
 
     l_arrive()
-    l_tot[...] = jnp.sum(l_xy[...], axis=0)
-    l_z[z] = l_tot[pl.ds(pl.multiple_of(core * 16, 16), 16), :]
+    l_z[z] = jnp.sum(l_xy[...], axis=0)
     lz_start, lz_arrive, lz_left = along_z(l_z.at[z], l_z, lzs, lzr)
     lz_start()
 
     g_arrive()
-    gram = unfold(jnp.sum(g_xy[...], axis=0))
+    g_half[...] = jnp.sum(g_xy[...], axis=0)
+    v_copy = remote(g_half, g_other, vs, vr)
+    v_copy.start()
+    e_arrive()
+    e_z[z] = jnp.sum(e_xy[...], axis=0)
+    ez_start, ez_arrive, ez_left = along_z(e_z.at[z], e_z, ezs, ezr)
+    ez_start()
+    v_copy.wait()
+    gram = halves(g_half[...], g_other[...])
     own_self = jnp.concatenate([noise_var * pivot_self, jnp.zeros((64, 64), f32)], axis=1)
     work = jnp.where(lane < 64, gram + own_self, jnp.where(lane == line + 64, 1.0, 0.0))
 
@@ -342,18 +365,15 @@
             work = work - jnp.where(line > k, factor, 0.0) * head
         return work
 
-    work = eliminate(work, 0, 24)
-    e_arrive()
-    e_z[z] = jnp.sum(e_xy[...], axis=0)
-    ez_start, ez_arrive, ez_left = along_z(e_z.at[z], e_z, ezs, ezr)
-    ez_start()
-    work = eliminate(work, 24, 64)
+    work = eliminate(work, 0, 64)
     diagonal = jnp.sum(jnp.where(lane == line, work, 0.0), axis=1, keepdims=True)
     lower_inv = pltpu.roll(work, 64, 1)[:, 0:64] * lax.rsqrt(diagonal)
     gram_inv = exact(lower_inv.T, lower_inv)
     mapped = exact(own_kernel_t, gram_inv)
 
-    loop(0, 15, lambda k: z_copy(k).wait_send())
+    loop(0, 8, lambda k: z_copy(k).wait_send())
+    loop(0, 4, lambda k: relay_up(k).wait_send())
+    loop(0, 3, lambda k: relay_down(k).wait_send())
     x_left()
     loop(0, 16, lambda p: w_copy(p).wait_send())
     q_left()
@@ -369,9 +389,7 @@
     u_copy.start()
     lz_left()
     u_copy.wait()
-    mine = l_half[...]
-    other = l_other[...]
-    projs = unfold(jnp.concatenate([jnp.where(core == 0, mine, other), jnp.where(core == 0, other, mine)], axis=0))
+    projs = halves(l_half[...], l_other[...])
     solved = exact(gram_inv, projs)
     spread = exact(mapped, projs)
 
@@ -426,6 +444,7 @@
     one = dma(())
     many = dma((16,))
     fold32 = vmem((16, 32, 128), f32)
+    fold16 = vmem((16, 16, 128), f32)
     flat32 = vmem((32, 128), f32)
     flat16 = vmem((16, 128), f32)
     flat1 = vmem((1, 128), f32)
@@ -437,11 +456,11 @@
         vmem((1024, 128), bf16), vmem((1024, 128), f32),
         fold32, fold32,
         vmem((16, 1, 128), f32), vmem((8, 128), f32), vmem((8, 128), f32), vmem((16, 8, 128), f32),
-        flat32, flat32, flat32, fold32,
-        flat32, flat32, flat32, fold32, flat32, vmem((16, 16, 128), f32), flat16, flat16,
+        flat32, flat16, flat16, fold16, flat16, flat16,
+        flat32, flat16, flat16, fold16, fold16, flat16, flat16,
         flat1, flat1, flat1, vmem((16, 1, 128), f32), vmem((16, 1, 128), f32),
         dma((6,)), many, many, many, many, many, many, many, many, many, many, one, one, many, many,
-        one, one, many, many, one, one, many, many, many, many, one, one, one, one, many, many, many, many,
+        one, one, many, many, one, one, one, one, many, many, many, many, one, one, one, one, many, many, many, many,
     ]
     result = pl.pallas_call(
         step_kernel,

time: 61.2 us -> 58.4 us (0.954)
  Pallas kernels: 60.3 us -> 57.5 us
    pallas_call x1, Pallas kernels: 58.8 us -> 56 us  [local(): pl.pallas_call(step_kernel, name='cg_step', out_shape=jax.ShapeDtypeStruc...]
where the time goes in v5:
time: 58.4 us; the launch traced here: 58.1 us
  Pallas kernels  57.5 us (98%)
  between operations  0.64 us (1%)
    pallas_call x1, Pallas kernels, local(): pl.pallas_call(step_kernel, name='cg_step', out_shape=jax.ShapeDtypeStruc...  56 us
    pallas_call x1, Pallas kernels, local(): pl.pallas_call(turn_kernel, name='turn', out_shape=(jax.ShapeDtypeStruct(...  1.47 us

profile of v5, /device:TPU:1, one launch (start us, length us, event | category | flops | bytes accessed | tf_op | source)
XLA Modules:
  0.0 58.1 jit_solution(2305814890248612334)
XLA Ops:
  0.6 56.0 %cg_step.1.result = f32[64,128]{1,0:T(8,128)} custom-call(bf16[64,64]{1,0:T(8,128)(2,1)} %feat_hbm.1, f32[1,64]{1,0:T(1,128)} %bitcast.2, s32[1,64]{1,0:T(1,128)} %bitcast.3, f32[32,64]{1,0:T(8,128)} %sol_hbm.1, f32[32,64]{1,0:T(8,128)} %res_hbm.1, f32[32,64]{1,0:T(8,128)} %dir_hbm.1), custom_call_target="tpu_custom_call" | custom-call | tf_op jit(solution)/shard_map/cg_step/pallas_call | solution.py:465
  56.7 1.5 %turn.1 = (f32[32,64]{1,0:T(8,128)}, f32[32,64]{1,0:T(8,128)}, f32[32,64]{1,0:T(8,128)}, f32[32,64]{1,0:T(8,128)}) custom-call(f32[64,128]{1,0:T(8,128)} %cg_step.1.result), custom_call_target="tpu_custom_call" | custom-call | tf_op jit(solution)/shard_map/turn/pallas_call | solution.py:476

commit v6 on v5

--- a/solution.py
+++ b/solution.py
@@ -24,6 +24,11 @@
         return carry
 
     lax.fori_loop(low, high, step, 0)
+
+
+def each(low, high, body):
+    for k in range(low, high):
+        body(jnp.int32(k))
 
 
 def exact(left, right, numbers=NN):
@@ -80,12 +85,12 @@
     feat_in, inv_in, piv_in, sol_in, res_in, dir_in,
     stage_a, stage_b,
     zbuf, zsib, xbuf, colm, acc,
-    part, part_xy,
+    part, part_xy, slopes, slopes_xy,
     q_z, q_own, q_sib, q_xy,
     g_own, g_sib, g_sum, g_xy, g_half, g_other,
     l_own, l_sib, l_sum, l_xy, l_z, l_half, l_other,
     e_own, e_sib, e_sum, e_xy, e_z,
-    in_sem, zs, zr, xs, xr, ws, wr, ps, pr, qs, qr, qcs, qcr, qxs, qxr,
+    in_sem, zs, zr, xs, xr, ws, wr, ps, pr, ds, dr, qs, qr, qcs, qcr, qxs, qxr,
     gs, gr, gxs, gxr, vs, vr, ls, lr, lxs, lxr, lzs, lzr, us, ur, es, er, exs, exr, ezs, ezr,
 ):
     row = lax.axis_index("row")
@@ -130,7 +135,7 @@
             return remote(src, buf.at[p], send.at[k], recv.at[p])
 
         return (
-            lambda: loop(0, 15, lambda k: copy(k).start()),
+            lambda: each(0, 15, lambda k: copy(k).start()),
             lambda: loop(0, 15, lambda k: arrival(k).wait_recv()),
             lambda: loop(0, 15, lambda k: copy(k).wait_send()),
         )
@@ -145,7 +150,7 @@
             return remote(src_of(p), buf.at[p], send.at[k], recv.at[p])
 
         return (
-            lambda: loop(1, 16, lambda k: copy(k).start()),
+            lambda: each(1, 16, lambda k: copy(k).start()),
             lambda: loop(1, 16, lambda k: arrival(k).wait_recv()),
             lambda: loop(1, 16, lambda k: copy(k).wait_send()),
         )
@@ -232,8 +237,8 @@
         w_copy(slot).start()
 
     x_start, x_arrive, x_left = over_xy(lambda p: xbuf.at[xy], xbuf, xs, xr)
-    loop(0, 8, lambda k: z_copy(k).start())
     q_start()
+    each(0, 8, lambda k: z_copy(k).start())
     x_start()
     w_copy(0).start()
 
@@ -251,9 +256,9 @@
         return zsib[group * 8 : group * 8 + 8]
 
     z_arrival(1)
-    loop(0, 4, lambda k: relay_up(k).start())
+    each(0, 4, lambda k: relay_up(k).start())
     z_arrival(2)
-    loop(0, 3, lambda k: relay_down(k).start())
+    each(0, 3, lambda k: relay_down(k).start())
     loop(1, 3, lambda slot: w_copy(slot).start())
     loop(3, 9, receive)
     x_arrive()
@@ -279,13 +284,26 @@
     total = acc[...] + tile(sibling_lines(1))
     acc[...] = total
 
-    total = total.reshape(16, 64, 128)
-    upper = total[:, 0:32].reshape(512, 128)
-    lower = total[:, 32:64].reshape(512, 128)
-    part[...] = (upper + pltpu.roll(lower, 64, 1)).reshape(16, 32, 128)
+    quarters = total.reshape(16, 4, 16, 128)
+    lane_q = iota((256, 128), 1)
+
+    def pack(first):
+        packed = jnp.zeros((256, 128), f32)
+        for q in range(4):
+            turned = pltpu.roll(quarters[:, q].reshape(256, 128), (32 * q - first) % 128, 1)
+            packed = jnp.where((lane_q >= 32 * q) & (lane_q < 32 * q + 32), turned, packed)
+        return packed.reshape(16, 16, 128)
+
+    def unpack(packed, first):
+        return jnp.concatenate([pltpu.roll(packed, (first - 32 * q) % 128, 1) for q in range(4)], axis=0)
+
+    part[...] = pack(0)
     part_xy[xy] = part[xy]
     s_start, s_arrive, s_left = over_xy(lambda p: part.at[p], part_xy, ps, pr)
     s_start()
+    slopes[...] = pack(32)
+    slopes_xy[xy] = slopes[xy]
+    d_start, d_arrive, d_left = over_xy(lambda p: slopes.at[p], slopes_xy, ds, dr)
 
     qx_arrive()
     lots = [q_xy[2 * pair] + q_xy[2 * pair + 1] for pair in range(8)]
@@ -320,9 +338,8 @@
     g_start()
 
     s_arrive()
-    images = unfold(jnp.sum(part_xy[...], axis=0))
+    images = unpack(jnp.sum(part_xy[...], axis=0), 0)
     image = jnp.where(lane < 32, images + noise_var * dir_t, 0.0)
-    slope = jnp.where((lane >= 32) & (lane < 64), images, 0.0)
     sums = jnp.sum(
         dir_t * image
         + pltpu.roll(res_t * image, 32, 1)
@@ -339,6 +356,7 @@
     e_xy[xy] = e_sum[...]
     e_start, e_arrive, e_left = over_xy(lambda p: e_sum, e_xy, exs, exr)
     e_start()
+    d_start()
 
     l_arrive()
     l_z[z] = jnp.sum(l_xy[...], axis=0)
@@ -349,10 +367,6 @@
     g_half[...] = jnp.sum(g_xy[...], axis=0)
     v_copy = remote(g_half, g_other, vs, vr)
     v_copy.start()
-    e_arrive()
-    e_z[z] = jnp.sum(e_xy[...], axis=0)
-    ez_start, ez_arrive, ez_left = along_z(e_z.at[z], e_z, ezs, ezr)
-    ez_start()
     v_copy.wait()
     gram = halves(g_half[...], g_other[...])
     own_self = jnp.concatenate([noise_var * pivot_self, jnp.zeros((64, 64), f32)], axis=1)
@@ -365,7 +379,12 @@
             work = work - jnp.where(line > k, factor, 0.0) * head
         return work
 
-    work = eliminate(work, 0, 64)
+    work = eliminate(work, 0, 20)
+    e_arrive()
+    e_z[z] = jnp.sum(e_xy[...], axis=0)
+    ez_start, ez_arrive, ez_left = along_z(e_z.at[z], e_z, ezs, ezr)
+    ez_start()
+    work = eliminate(work, 20, 64)
     diagonal = jnp.sum(jnp.where(lane == line, work, 0.0), axis=1, keepdims=True)
     lower_inv = pltpu.roll(work, 64, 1)[:, 0:64] * lax.rsqrt(diagonal)
     gram_inv = exact(lower_inv.T, lower_inv)
@@ -382,6 +401,9 @@
     g_left()
     l_left()
     e_left()
+    d_arrive()
+    d_left()
+    slope = unpack(jnp.sum(slopes_xy[...], axis=0), 96)
 
     lz_arrive()
     l_half[...] = jnp.sum(l_z[...], axis=0)
@@ -423,7 +445,7 @@
         jnp.where(
             lane < 64,
             pltpu.roll(residual_new, 32, 1),
-            jnp.where(lane < 96, pltpu.roll(direction_new, 64, 1), pltpu.roll(slope, 64, 1)),
+            jnp.where(lane < 96, pltpu.roll(direction_new, 64, 1), slope),
         ),
     )
 
@@ -443,7 +465,6 @@
     dma = pltpu.SemaphoreType.DMA
     one = dma(())
     many = dma((16,))
-    fold32 = vmem((16, 32, 128), f32)
     fold16 = vmem((16, 16, 128), f32)
     flat32 = vmem((32, 128), f32)
     flat16 = vmem((16, 128), f32)
@@ -454,12 +475,12 @@
         vmem((128, 128), f32), vmem((128, 128), f32),
         vmem((16, 48, 128), bf16), vmem((16, 48, 128), bf16), vmem((16, 64, 128), bf16),
         vmem((1024, 128), bf16), vmem((1024, 128), f32),
-        fold32, fold32,
+        fold16, fold16, fold16, fold16,
         vmem((16, 1, 128), f32), vmem((8, 128), f32), vmem((8, 128), f32), vmem((16, 8, 128), f32),
         flat32, flat16, flat16, fold16, flat16, flat16,
         flat32, flat16, flat16, fold16, fold16, flat16, flat16,
         flat1, flat1, flat1, vmem((16, 1, 128), f32), vmem((16, 1, 128), f32),
-        dma((6,)), many, many, many, many, many, many, many, many, many, many, one, one, many, many,
+        dma((6,)), many, many, many, many, many, many, many, many, many, many, many, many, one, one, many, many,
         one, one, many, many, one, one, one, one, many, many, many, many, one, one, one, one, many, many, many, many,
     ]
     result = pl.pallas_call(

time: 58.4 us -> 59.5 us (1.019)
  Pallas kernels: 57.5 us -> 58.6 us
    pallas_call x1, Pallas kernels: 56 us -> 57.2 us  [local(): pl.pallas_call(step_kernel, name='cg_step', out_shape=jax.ShapeDtypeStruc...]
where the time goes in v6:
time: 59.5 us; the launch traced here: 59.3 us
  Pallas kernels  58.6 us (98%)
  between operations  0.64 us (1%)
    pallas_call x1, Pallas kernels, local(): pl.pallas_call(step_kernel, name='cg_step', out_shape=jax.ShapeDtypeStruc...  57.2 us
    pallas_call x1, Pallas kernels, local(): pl.pallas_call(turn_kernel, name='turn', out_shape=(jax.ShapeDtypeStruct(...  1.47 us

profile of v6, /device:TPU:1, one launch (start us, length us, event | category | flops | bytes accessed | tf_op | source)
XLA Modules:
  0.0 59.3 jit_solution(3140572570331116777)
XLA Ops:
  0.6 57.2 %cg_step.1.result = f32[64,128]{1,0:T(8,128)} custom-call(bf16[64,64]{1,0:T(8,128)(2,1)} %feat_hbm.1, f32[1,64]{1,0:T(1,128)} %bitcast.2, s32[1,64]{1,0:T(1,128)} %bitcast.3, f32[32,64]{1,0:T(8,128)} %sol_hbm.1, f32[32,64]{1,0:T(8,128)} %res_hbm.1, f32[32,64]{1,0:T(8,128)} %dir_hbm.1), custom_call_target="tpu_custom_call" | custom-call | tf_op jit(solution)/shard_map/cg_step/pallas_call | solution.py:486
  57.8 1.5 %turn.1 = (f32[32,64]{1,0:T(8,128)}, f32[32,64]{1,0:T(8,128)}, f32[32,64]{1,0:T(8,128)}, f32[32,64]{1,0:T(8,128)}) custom-call(f32[64,128]{1,0:T(8,128)} %cg_step.1.result), custom_call_target="tpu_custom_call" | custom-call | tf_op jit(solution)/shard_map/turn/pallas_call | solution.py:497

commit v7 on v6

--- a/solution.py
+++ b/solution.py
@@ -126,34 +126,19 @@
         second = jnp.where(core == 0, other, mine)
         return unfold(jnp.concatenate([first, second], axis=0))
 
+    def exchange(count, copy, buf, send, recv):
+        whole = remote(buf.at[0:count], buf.at[0:count], send, recv)
+        return (lambda: each(0, count, lambda k: copy(k).start())), whole.wait_recv, whole.wait_send
+
     def along_z(src, buf, send, recv):
-        def copy(k):
-            return remote(src, buf.at[z], send.at[k], recv.at[z], dev(z_peer(k), xy, core))
-
-        def arrival(k):
-            p = z_peer(k)
-            return remote(src, buf.at[p], send.at[k], recv.at[p])
-
-        return (
-            lambda: each(0, 15, lambda k: copy(k).start()),
-            lambda: loop(0, 15, lambda k: arrival(k).wait_recv()),
-            lambda: loop(0, 15, lambda k: copy(k).wait_send()),
-        )
+        return exchange(15, lambda k: remote(src, buf.at[z], send, recv, dev(z_peer(k), xy, core)), buf, send, recv)
 
     def over_xy(src_of, buf, send, recv):
         def copy(k):
-            p = xy_peer(k)
-            return remote(src_of(p), buf.at[xy], send.at[k], recv.at[xy], dev(z, p, core))
-
-        def arrival(k):
-            p = xy_peer(k)
-            return remote(src_of(p), buf.at[p], send.at[k], recv.at[p])
-
-        return (
-            lambda: each(1, 16, lambda k: copy(k).start()),
-            lambda: loop(1, 16, lambda k: arrival(k).wait_recv()),
-            lambda: loop(1, 16, lambda k: copy(k).wait_send()),
-        )
+            p = xy_peer(k + 1)
+            return remote(src_of(p), buf.at[xy], send, recv, dev(z, p, core))
+
+        return exchange(15, copy, buf, send, recv)
 
     barrier = pltpu.get_barrier_semaphore()
 
@@ -218,29 +203,33 @@
         return dev(lax.rem(z + jnp.where(lax.rem(k, 2) == 0, far, 16 - far), 16), xy, core)
 
     def z_copy(k):
-        return remote(zbuf.at[0], zbuf.at[k + 1], zs.at[k], zr.at[k], z_near(k))
+        at = min(k, 2)
+        return remote(zbuf.at[0], zbuf.at[k + 1], zs, zr.at[at], z_near(jnp.int32(k)))
 
     def relay_up(k):
-        return remote(zbuf.at[1], zbuf.at[k + 9], zs.at[k + 8], zr.at[k + 8], dev(lax.rem(z + 4 - k, 16), xy, core))
+        return remote(zbuf.at[1], zbuf.at[k + 9], zs, zr.at[3], dev(lax.rem(z + 4 - k, 16), xy, core))
 
     def relay_down(k):
-        return remote(zbuf.at[2], zbuf.at[k + 13], zs.at[k + 12], zr.at[k + 12], dev(lax.rem(z + 13 + k, 16), xy, core))
-
-    def z_arrival(slot):
-        remote(zbuf.at[0], zbuf.at[slot], zs.at[slot - 1], zr.at[slot - 1]).wait_recv()
-
-    def w_copy(slot):
-        return remote(zbuf.at[slot], zsib.at[slot], ws.at[slot], wr.at[slot])
-
-    def receive(slot):
-        z_arrival(slot)
-        w_copy(slot).start()
+        return remote(zbuf.at[2], zbuf.at[k + 13], zs, zr.at[3], dev(lax.rem(z + 13 + k, 16), xy, core))
+
+    def z_arrival(slots, at):
+        remote(zbuf.at[slots], zbuf.at[slots], zs, zr.at[at]).wait_recv()
+
+    def z_left():
+        remote(zbuf.at[0:15], zbuf.at[0:15], zs, zr.at[0]).wait_send()
+
+    shared = [
+        remote(zbuf.at[slots], zsib.at[slots], ws.at[n], wr.at[n])
+        for n, slots in enumerate((pl.ds(0, 3), pl.ds(3, 6), pl.ds(9, 7)))
+    ]
 
     x_start, x_arrive, x_left = over_xy(lambda p: xbuf.at[xy], xbuf, xs, xr)
+    for k in range(2):
+        z_copy(k).start()
     q_start()
-    each(0, 8, lambda k: z_copy(k).start())
+    for k in range(2, 8):
+        z_copy(k).start()
     x_start()
-    w_copy(0).start()
 
     def tile(blocks, keep=None):
         cols, plain, slope = unfold_block(blocks)
@@ -251,16 +240,15 @@
         images = jnp.dot(value.astype(bf16), plain, preferred_element_type=f32)
         return images + jnp.dot((value * half).astype(bf16), slope, preferred_element_type=f32)
 
-    def sibling_lines(group):
-        loop(group * 8, group * 8 + 8, lambda slot: w_copy(slot).wait_recv())
-        return zsib[group * 8 : group * 8 + 8]
-
-    z_arrival(1)
-    each(0, 4, lambda k: relay_up(k).start())
-    z_arrival(2)
-    each(0, 3, lambda k: relay_down(k).start())
-    loop(1, 3, lambda slot: w_copy(slot).start())
-    loop(3, 9, receive)
+    z_arrival(pl.ds(1, 1), 0)
+    for k in range(4):
+        relay_up(k).start()
+    z_arrival(pl.ds(2, 1), 1)
+    for k in range(3):
+        relay_down(k).start()
+    shared[0].start()
+    z_arrival(pl.ds(3, 6), 2)
+    shared[1].start()
     x_arrive()
     acc[...] = tile(zbuf[0:8], 0)
 
@@ -274,14 +262,18 @@
     qc_copy = remote(q_own, q_sib, qcs, qcr)
     qc_copy.start()
 
-    acc[...] += tile(sibling_lines(0))
+    shared[0].wait_recv()
+    shared[1].wait_recv()
+    acc[...] += tile(zsib[0:8])
     qc_copy.wait()
     q_xy[xy] = q_own[...] + q_sib[...]
     qx_start, qx_arrive, qx_left = over_xy(lambda p: q_xy.at[xy], q_xy, qxs, qxr)
     qx_start()
-    loop(9, 16, receive)
+    z_arrival(pl.ds(9, 7), 3)
+    shared[2].start()
     acc[...] += tile(zbuf[8:16], 1)
-    total = acc[...] + tile(sibling_lines(1))
+    shared[2].wait_recv()
+    total = acc[...] + tile(zsib[8:16])
     acc[...] = total
 
     quarters = total.reshape(16, 4, 16, 128)
@@ -351,6 +343,13 @@
     e_own[...] = sums
     e_copy = remote(e_own, e_sib, es, er)
     e_copy.start()
+    z_left()
+    for copy in shared:
+        copy.wait_send()
+    x_left()
+    q_left()
+    qx_left()
+    s_left()
     e_copy.wait()
     e_sum[...] = e_own[...] + e_sib[...]
     e_xy[xy] = e_sum[...]
@@ -367,6 +366,8 @@
     g_half[...] = jnp.sum(g_xy[...], axis=0)
     v_copy = remote(g_half, g_other, vs, vr)
     v_copy.start()
+    g_left()
+    l_left()
     v_copy.wait()
     gram = halves(g_half[...], g_other[...])
     own_self = jnp.concatenate([noise_var * pivot_self, jnp.zeros((64, 64), f32)], axis=1)
@@ -390,16 +391,6 @@
     gram_inv = exact(lower_inv.T, lower_inv)
     mapped = exact(own_kernel_t, gram_inv)
 
-    loop(0, 8, lambda k: z_copy(k).wait_send())
-    loop(0, 4, lambda k: relay_up(k).wait_send())
-    loop(0, 3, lambda k: relay_down(k).wait_send())
-    x_left()
-    loop(0, 16, lambda p: w_copy(p).wait_send())
-    q_left()
-    qx_left()
-    s_left()
-    g_left()
-    l_left()
     e_left()
     d_arrive()
     d_left()
@@ -464,7 +455,6 @@
     vmem = pltpu.VMEM
     dma = pltpu.SemaphoreType.DMA
     one = dma(())
-    many = dma((16,))
     fold16 = vmem((16, 16, 128), f32)
     flat32 = vmem((32, 128), f32)
     flat16 = vmem((16, 128), f32)
@@ -480,8 +470,7 @@
         flat32, flat16, flat16, fold16, flat16, flat16,
         flat32, flat16, flat16, fold16, fold16, flat16, flat16,
         flat1, flat1, flat1, vmem((16, 1, 128), f32), vmem((16, 1, 128), f32),
-        dma((6,)), many, many, many, many, many, many, many, many, many, many, many, many, one, one, many, many,
-        one, one, many, many, one, one, one, one, many, many, many, many, one, one, one, one, many, many, many, many,
+        dma((6,)), one, dma((4,)), one, one, dma((3,)), dma((3,)), *[one] * 30,
     ]
     result = pl.pallas_call(
         step_kernel,

time: 59.5 us -> 55.7 us (0.936)
  Pallas kernels: 58.6 us -> 54.8 us
    pallas_call x1, Pallas kernels: 57.2 us -> 53.3 us  [local(): pl.pallas_call(step_kernel, name='cg_step', out_shape=jax.ShapeDtypeStruc...]
where the time goes in v7:
time: 55.7 us; the launch traced here: 55.5 us
  Pallas kernels  54.8 us (98%)
  between operations  0.64 us (1%)
    pallas_call x1, Pallas kernels, local(): pl.pallas_call(step_kernel, name='cg_step', out_shape=jax.ShapeDtypeStruc...  53.3 us
    pallas_call x1, Pallas kernels, local(): pl.pallas_call(turn_kernel, name='turn', out_shape=(jax.ShapeDtypeStruct(...  1.47 us

profile of v7, /device:TPU:1, one launch (start us, length us, event | category | flops | bytes accessed | tf_op | source)
XLA Modules:
  0.0 55.5 jit_solution(16484581637906362415)
XLA Ops:
  0.6 53.3 %cg_step.1.result = f32[64,128]{1,0:T(8,128)} custom-call(bf16[64,64]{1,0:T(8,128)(2,1)} %feat_hbm.1, f32[1,64]{1,0:T(1,128)} %bitcast.2, s32[1,64]{1,0:T(1,128)} %bitcast.3, f32[32,64]{1,0:T(8,128)} %sol_hbm.1, f32[32,64]{1,0:T(8,128)} %res_hbm.1, f32[32,64]{1,0:T(8,128)} %dir_hbm.1), custom_call_target="tpu_custom_call" | custom-call | tf_op jit(solution)/shard_map/cg_step/pallas_call | solution.py:475
  54.0 1.5 %turn.1 = (f32[32,64]{1,0:T(8,128)}, f32[32,64]{1,0:T(8,128)}, f32[32,64]{1,0:T(8,128)}, f32[32,64]{1,0:T(8,128)}) custom-call(f32[64,128]{1,0:T(8,128)} %cg_step.1.result), custom_call_target="tpu_custom_call" | custom-call | tf_op jit(solution)/shard_map/turn/pallas_call | solution.py:486

commit v8 on v7

--- a/solution.py
+++ b/solution.py
@@ -355,12 +355,16 @@
     e_xy[xy] = e_sum[...]
     e_start, e_arrive, e_left = over_xy(lambda p: e_sum, e_xy, exs, exr)
     e_start()
-    d_start()
 
     l_arrive()
     l_z[z] = jnp.sum(l_xy[...], axis=0)
     lz_start, lz_arrive, lz_left = along_z(l_z.at[z], l_z, lzs, lzr)
     lz_start()
+    e_arrive()
+    e_z[z] = jnp.sum(e_xy[...], axis=0)
+    ez_start, ez_arrive, ez_left = along_z(e_z.at[z], e_z, ezs, ezr)
+    ez_start()
+    d_start()
 
     g_arrive()
     g_half[...] = jnp.sum(g_xy[...], axis=0)
@@ -373,19 +377,19 @@
     own_self = jnp.concatenate([noise_var * pivot_self, jnp.zeros((64, 64), f32)], axis=1)
     work = jnp.where(lane < 64, gram + own_self, jnp.where(lane == line + 64, 1.0, 0.0))
 
-    def eliminate(work, low, high):
-        for k in range(low, high):
-            head = work[k : k + 1, :]
-            factor = work[:, k : k + 1] * (1.0 / head[:, k : k + 1])
-            work = work - jnp.where(line > k, factor, 0.0) * head
-        return work
-
-    work = eliminate(work, 0, 20)
-    e_arrive()
-    e_z[z] = jnp.sum(e_xy[...], axis=0)
-    ez_start, ez_arrive, ez_left = along_z(e_z.at[z], e_z, ezs, ezr)
-    ez_start()
-    work = eliminate(work, 20, 64)
+    done = []
+    for panel in range(8):
+        count = 64 - 8 * panel
+        below = iota((count, 128), 0)
+        cols = [jnp.broadcast_to(work[:, 8 * panel + j : 8 * panel + j + 1], (count, 128)) for j in range(8)]
+        for k in range(8):
+            factor = jnp.where(below > k, cols[k] * (1.0 / cols[k][k : k + 1]), 0.0)
+            work = work - factor * work[k : k + 1]
+            for j in range(k + 1, 8):
+                cols[j] = cols[j] - factor * cols[j][k : k + 1]
+        done.append(work[0:8])
+        work = work[8:]
+    work = jnp.concatenate(done, axis=0)
     diagonal = jnp.sum(jnp.where(lane == line, work, 0.0), axis=1, keepdims=True)
     lower_inv = pltpu.roll(work, 64, 1)[:, 0:64] * lax.rsqrt(diagonal)
     gram_inv = exact(lower_inv.T, lower_inv)

time: 55.7 us -> 51.6 us (0.926)
  Pallas kernels: 54.8 us -> 50.7 us
    pallas_call x1, Pallas kernels: 53.3 us -> 49.3 us  [local(): pl.pallas_call(step_kernel, name='cg_step', out_shape=jax.ShapeDtypeStruc...]
where the time goes in v8:
time: 51.6 us; the launch traced here: 51.4 us
  Pallas kernels  50.7 us (98%)
  between operations  0.64 us (1%)
    pallas_call x1, Pallas kernels, local(): pl.pallas_call(step_kernel, name='cg_step', out_shape=jax.ShapeDtypeStruc...  49.3 us
    pallas_call x1, Pallas kernels, local(): pl.pallas_call(turn_kernel, name='turn', out_shape=(jax.ShapeDtypeStruct(...  1.47 us

profile of v8, /device:TPU:1, one launch (start us, length us, event | category | flops | bytes accessed | tf_op | source)
XLA Modules:
  0.0 51.4 jit_solution(12598317108894068807)
XLA Ops:
  0.6 49.3 %cg_step.1.result = f32[64,128]{1,0:T(8,128)} custom-call(bf16[64,64]{1,0:T(8,128)(2,1)} %feat_hbm.1, f32[1,64]{1,0:T(1,128)} %bitcast.2, s32[1,64]{1,0:T(1,128)} %bitcast.3, f32[32,64]{1,0:T(8,128)} %sol_hbm.1, f32[32,64]{1,0:T(8,128)} %res_hbm.1, f32[32,64]{1,0:T(8,128)} %dir_hbm.1), custom_call_target="tpu_custom_call" | custom-call | tf_op jit(solution)/shard_map/cg_step/pallas_call | solution.py:479
  49.9 1.5 %turn.1 = (f32[32,64]{1,0:T(8,128)}, f32[32,64]{1,0:T(8,128)}, f32[32,64]{1,0:T(8,128)}, f32[32,64]{1,0:T(8,128)}) custom-call(f32[64,128]{1,0:T(8,128)} %cg_step.1.result), custom_call_target="tpu_custom_call" | custom-call | tf_op jit(solution)/shard_map/turn/pallas_call | solution.py:490

commit v9 on v8

--- a/solution.py
+++ b/solution.py
@@ -109,6 +109,10 @@
     def z_peer(k):
         return lax.rem(z + z_shift(k), 16)
 
+    def z_near(k):
+        far = 4 - k // 2
+        return dev(lax.rem(z + jnp.where(lax.rem(k, 2) == 0, far, 16 - far), 16), xy, core)
+
     def xy_peer(k):
         return lax.rem(xy + k, 16)
 
@@ -145,7 +149,7 @@
     def greet(where):
         pl.semaphore_signal(barrier, inc=1, device_id=where, device_id_type=MESH)
 
-    loop(0, 15, lambda k: greet(dev(z_peer(k), xy, core)))
+    loop(0, 8, lambda k: greet(z_near(k)))
     loop(1, 16, lambda k: greet(dev(z, xy_peer(k), core)))
     greet(sibling)
 
@@ -194,13 +198,7 @@
     ).astype(bf16)
     xbuf[xy] = own_row
 
-    pl.semaphore_wait(barrier, 31)
-
-    q_start, q_arrive, q_left = along_z(q_z.at[z], q_z, qs, qr)
-
-    def z_near(k):
-        far = 4 - k // 2
-        return dev(lax.rem(z + jnp.where(lax.rem(k, 2) == 0, far, 16 - far), 16), xy, core)
+    pl.semaphore_wait(barrier, 24)
 
     def z_copy(k):
         at = min(k, 2)
@@ -211,6 +209,23 @@
 
     def relay_down(k):
         return remote(zbuf.at[2], zbuf.at[k + 13], zs, zr.at[3], dev(lax.rem(z + 13 + k, 16), xy, core))
+
+    def q_copy(k):
+        return remote(q_z.at[z], q_z.at[z], qs, qr.at[min(k, 2)], z_near(jnp.int32(k)))
+
+    def q_up(k):
+        p = lax.rem(z + 12, 16)
+        return remote(q_z.at[p], q_z.at[p], qs, qr.at[3], dev(lax.rem(z + 4 - k, 16), xy, core))
+
+    def q_down(k):
+        p = lax.rem(z + 4, 16)
+        return remote(q_z.at[p], q_z.at[p], qs, qr.at[3], dev(lax.rem(z + 13 + k, 16), xy, core))
+
+    def q_arrival(count, at):
+        remote(q_z.at[0:count], q_z.at[0:count], qs, qr.at[at]).wait_recv()
+
+    def q_left():
+        remote(q_z.at[0:15], q_z.at[0:15], qs, qr.at[0]).wait_send()
 
     def z_arrival(slots, at):
         remote(zbuf.at[slots], zbuf.at[slots], zs, zr.at[at]).wait_recv()
@@ -226,7 +241,9 @@
     x_start, x_arrive, x_left = over_xy(lambda p: xbuf.at[xy], xbuf, xs, xr)
     for k in range(2):
         z_copy(k).start()
-    q_start()
+        q_copy(k).start()
+    for k in range(2, 8):
+        q_copy(k).start()
     for k in range(2, 8):
         z_copy(k).start()
     x_start()
@@ -240,9 +257,15 @@
         images = jnp.dot(value.astype(bf16), plain, preferred_element_type=f32)
         return images + jnp.dot((value * half).astype(bf16), slope, preferred_element_type=f32)
 
+    q_arrival(1, 0)
+    for k in range(4):
+        q_up(k).start()
     z_arrival(pl.ds(1, 1), 0)
     for k in range(4):
         relay_up(k).start()
+    q_arrival(1, 1)
+    for k in range(3):
+        q_down(k).start()
     z_arrival(pl.ds(2, 1), 1)
     for k in range(3):
         relay_down(k).start()
@@ -252,7 +275,8 @@
     x_arrive()
     acc[...] = tile(zbuf[0:8], 0)
 
-    q_arrive()
+    q_arrival(6, 2)
+    q_arrival(7, 3)
     line8 = iota((8, 128), 0)
     found = jnp.zeros((8, 128), f32)
     for low in range(4):
@@ -474,7 +498,7 @@
         flat32, flat16, flat16, fold16, flat16, flat16,
         flat32, flat16, flat16, fold16, fold16, flat16, flat16,
         flat1, flat1, flat1, vmem((16, 1, 128), f32), vmem((16, 1, 128), f32),
-        dma((6,)), one, dma((4,)), one, one, dma((3,)), dma((3,)), *[one] * 30,
+        dma((6,)), one, dma((4,)), one, one, dma((3,)), dma((3,)), *[one] * 4, one, dma((4,)), *[one] * 24,
     ]
     result = pl.pallas_call(
         step_kernel,

time: 51.6 us -> 52.5 us (1.017)
  Pallas kernels: 50.7 us -> 51.6 us
    pallas_call x1, Pallas kernels: 49.3 us -> 50.1 us  [local(): pl.pallas_call(step_kernel, name='cg_step', out_shape=jax.ShapeDtypeStruc...]
where the time goes in v9:
time: 52.5 us; the launch traced here: 52.2 us
  Pallas kernels  51.6 us (98%)
  between operations  0.64 us (1%)
    pallas_call x1, Pallas kernels, local(): pl.pallas_call(step_kernel, name='cg_step', out_shape=jax.ShapeDtypeStruc...  50.1 us
    pallas_call x1, Pallas kernels, local(): pl.pallas_call(turn_kernel, name='turn', out_shape=(jax.ShapeDtypeStruct(...  1.47 us

profile of v9, /device:TPU:1, one launch (start us, length us, event | category | flops | bytes accessed | tf_op | source)
XLA Modules:
  0.0 52.2 jit_solution(8912913431703961380)
XLA Ops:
  0.6 50.1 %cg_step.1.result = f32[64,128]{1,0:T(8,128)} custom-call(bf16[64,64]{1,0:T(8,128)(2,1)} %feat_hbm.1, f32[1,64]{1,0:T(1,128)} %bitcast.2, s32[1,64]{1,0:T(1,128)} %bitcast.3, f32[32,64]{1,0:T(8,128)} %sol_hbm.1, f32[32,64]{1,0:T(8,128)} %res_hbm.1, f32[32,64]{1,0:T(8,128)} %dir_hbm.1), custom_call_target="tpu_custom_call" | custom-call | tf_op jit(solution)/shard_map/cg_step/pallas_call | solution.py:503
  50.7 1.5 %turn.1 = (f32[32,64]{1,0:T(8,128)}, f32[32,64]{1,0:T(8,128)}, f32[32,64]{1,0:T(8,128)}, f32[32,64]{1,0:T(8,128)}) custom-call(f32[64,128]{1,0:T(8,128)} %cg_step.1.result), custom_call_target="tpu_custom_call" | custom-call | tf_op jit(solution)/shard_map/turn/pallas_call | solution.py:514

commit v10 on v8

--- a/solution.py
+++ b/solution.py
@@ -84,7 +84,7 @@
     result,
     feat_in, inv_in, piv_in, sol_in, res_in, dir_in,
     stage_a, stage_b,
-    zbuf, zsib, xbuf, colm, acc,
+    zall, xbuf, colm, acc,
     part, part_xy, slopes, slopes_xy,
     q_z, q_own, q_sib, q_xy,
     g_own, g_sib, g_sum, g_xy, g_half, g_other,
@@ -93,6 +93,8 @@
     in_sem, zs, zr, xs, xr, ws, wr, ps, pr, ds, dr, qs, qr, qcs, qcr, qxs, qxr,
     gs, gr, gxs, gxr, vs, vr, ls, lr, lxs, lxr, lzs, lzr, us, ur, es, er, exs, exr, ezs, ezr,
 ):
+    zbuf = zall.at[0]
+    zsib = zall.at[1]
     row = lax.axis_index("row")
     col = lax.axis_index("col")
     xy = lax.rem(row, 16)
@@ -231,15 +233,6 @@
         z_copy(k).start()
     x_start()
 
-    def tile(blocks, keep=None):
-        cols, plain, slope = unfold_block(blocks)
-        if keep is not None:
-            colm[keep * 512 : keep * 512 + 512, :] = cols
-        half = lax.dot_general(xbuf[...].reshape(1024, 128), cols, NT, preferred_element_type=f32)
-        value = jnp.exp(half)
-        images = jnp.dot(value.astype(bf16), plain, preferred_element_type=f32)
-        return images + jnp.dot((value * half).astype(bf16), slope, preferred_element_type=f32)
-
     z_arrival(pl.ds(1, 1), 0)
     for k in range(4):
         relay_up(k).start()
@@ -250,31 +243,47 @@
     z_arrival(pl.ds(3, 6), 2)
     shared[1].start()
     x_arrive()
-    acc[...] = tile(zbuf[0:8], 0)
-
-    q_arrive()
-    line8 = iota((8, 128), 0)
-    found = jnp.zeros((8, 128), f32)
-    for low in range(4):
-        lot = q_z[low] + q_z[4 + low] + q_z[8 + low] + q_z[12 + low]
-        found = found + jnp.where(line8 == lax.rem(xy, 2) * 4 + low, lot, 0.0)
-    q_own[...] = found
+    acc[...] = jnp.zeros((1024, 128), f32)
     qc_copy = remote(q_own, q_sib, qcs, qcr)
-    qc_copy.start()
-
-    shared[0].wait_recv()
-    shared[1].wait_recv()
-    acc[...] += tile(zsib[0:8])
-    qc_copy.wait()
-    q_xy[xy] = q_own[...] + q_sib[...]
     qx_start, qx_arrive, qx_left = over_xy(lambda p: q_xy.at[xy], q_xy, qxs, qxr)
-    qx_start()
-    z_arrival(pl.ds(9, 7), 3)
-    shared[2].start()
-    acc[...] += tile(zbuf[8:16], 1)
-    shared[2].wait_recv()
-    total = acc[...] + tile(zsib[8:16])
-    acc[...] = total
+
+    def tile(step):
+        @pl.when(step == 1)
+        def _():
+            q_arrive()
+            line8 = iota((8, 128), 0)
+            found = jnp.zeros((8, 128), f32)
+            for low in range(4):
+                lot = q_z[low] + q_z[4 + low] + q_z[8 + low] + q_z[12 + low]
+                found = found + jnp.where(line8 == lax.rem(xy, 2) * 4 + low, lot, 0.0)
+            q_own[...] = found
+            qc_copy.start()
+            shared[0].wait_recv()
+            shared[1].wait_recv()
+
+        @pl.when(step == 2)
+        def _():
+            qc_copy.wait()
+            q_xy[xy] = q_own[...] + q_sib[...]
+            qx_start()
+            z_arrival(pl.ds(9, 7), 3)
+            shared[2].start()
+
+        @pl.when(step == 3)
+        def _():
+            shared[2].wait_recv()
+
+        side = lax.rem(step, 2)
+        group = step // 2
+        cols, plain, slope = unfold_block(zall[side, pl.ds(pl.multiple_of(group * 8, 8), 8)])
+        colm[side, pl.ds(pl.multiple_of(group * 512, 512), 512), :] = cols
+        half = lax.dot_general(xbuf[...].reshape(1024, 128), cols, NT, preferred_element_type=f32)
+        value = jnp.exp(half)
+        images = jnp.dot(value.astype(bf16), plain, preferred_element_type=f32)
+        acc[...] += images + jnp.dot((value * half).astype(bf16), slope, preferred_element_type=f32)
+
+    loop(0, 4, tile)
+    total = acc[...]
 
     quarters = total.reshape(16, 4, 16, 128)
     lane_q = iota((256, 128), 1)
@@ -310,7 +319,7 @@
     l_copy = remote(l_own.at[given], l_sib, ls, lr)
     l_copy.start()
 
-    line_kernel = kernel_of(pivot_row, colm[...])
+    line_kernel = kernel_of(pivot_row, colm[0])
     gram_part = exact(line_kernel, line_kernel, NT)
     wide = jnp.concatenate([gram_part, jnp.zeros((64, 64), f32)], axis=1)
     g_own[...] = wide[0:32] + pltpu.roll(wide[32:64], 64, 1)
@@ -467,8 +476,8 @@
         vmem((64, 64), bf16), vmem((1, 64), f32), vmem((1, 64), jnp.int32),
         vmem((32, 64), f32), vmem((32, 64), f32), vmem((32, 64), f32),
         vmem((128, 128), f32), vmem((128, 128), f32),
-        vmem((16, 48, 128), bf16), vmem((16, 48, 128), bf16), vmem((16, 64, 128), bf16),
-        vmem((1024, 128), bf16), vmem((1024, 128), f32),
+        vmem((2, 16, 48, 128), bf16), vmem((16, 64, 128), bf16),
+        vmem((2, 1024, 128), bf16), vmem((1024, 128), f32),
         fold16, fold16, fold16, fold16,
         vmem((16, 1, 128), f32), vmem((8, 128), f32), vmem((8, 128), f32), vmem((16, 8, 128), f32),
         flat32, flat16, flat16, fold16, flat16, flat16,

time: 51.6 us -> 51.1 us (level)
  Pallas kernels: 50.7 us -> 50.1 us
    pallas_call x1, Pallas kernels: 49.3 us -> 48.7 us  [local(): pl.pallas_call(step_kernel, name='cg_step', out_shape=jax.ShapeDtypeStruc...]
where the time goes in v10:
time: 51.1 us; the launch traced here: 50.8 us
  Pallas kernels  50.1 us (98%)
  between operations  0.64 us (1%)
    pallas_call x1, Pallas kernels, local(): pl.pallas_call(step_kernel, name='cg_step', out_shape=jax.ShapeDtypeStruc...  48.7 us
    pallas_call x1, Pallas kernels, local(): pl.pallas_call(turn_kernel, name='turn', out_shape=(jax.ShapeDtypeStruct(...  1.47 us

profile of v10, /device:TPU:1, one launch (start us, length us, event | category | flops | bytes accessed | tf_op | source)
XLA Modules:
  0.0 50.8 jit_solution(9288029884554254688)
XLA Ops:
  0.6 48.7 %cg_step.1.result = f32[64,128]{1,0:T(8,128)} custom-call(bf16[64,64]{1,0:T(8,128)(2,1)} %feat_hbm.1, f32[1,64]{1,0:T(1,128)} %bitcast.2, s32[1,64]{1,0:T(1,128)} %bitcast.3, f32[32,64]{1,0:T(8,128)} %sol_hbm.1, f32[32,64]{1,0:T(8,128)} %res_hbm.1, f32[32,64]{1,0:T(8,128)} %dir_hbm.1), custom_call_target="tpu_custom_call" | custom-call | tf_op jit(solution)/shard_map/cg_step/pallas_call | solution.py:488
  49.3 1.5 %turn.1 = (f32[32,64]{1,0:T(8,128)}, f32[32,64]{1,0:T(8,128)}, f32[32,64]{1,0:T(8,128)}, f32[32,64]{1,0:T(8,128)}) custom-call(f32[64,128]{1,0:T(8,128)} %cg_step.1.result), custom_call_target="tpu_custom_call" | custom-call | tf_op jit(solution)/shard_map/turn/pallas_call | solution.py:499

commit v11 on v10

--- a/solution.py
+++ b/solution.py
@@ -302,8 +302,6 @@
     part_xy[xy] = part[xy]
     s_start, s_arrive, s_left = over_xy(lambda p: part.at[p], part_xy, ps, pr)
     s_start()
-    slopes[...] = pack(32)
-    slopes_xy[xy] = slopes[xy]
     d_start, d_arrive, d_left = over_xy(lambda p: slopes.at[p], slopes_xy, ds, dr)
 
     qx_arrive()
@@ -325,6 +323,8 @@
     g_own[...] = wide[0:32] + pltpu.roll(wide[32:64], 64, 1)
     g_copy = remote(g_own.at[given], g_sib, gs, gr)
     g_copy.start()
+    slopes[...] = pack(32)
+    slopes_xy[xy] = slopes[xy]
     l_copy.wait()
     l_sum[...] = l_own[kept, :] + l_sib[...]
     l_xy[xy] = l_sum[...]

time: 51.1 us -> 51.1 us (level)
  no operation moved by 1% of the time
where the time goes in v11:
time: 51.1 us; the launch traced here: 50.7 us
  Pallas kernels  50 us (98%)
  between operations  0.64 us (1%)
    pallas_call x1, Pallas kernels, local(): pl.pallas_call(step_kernel, name='cg_step', out_shape=jax.ShapeDtypeStruc...  48.6 us
    pallas_call x1, Pallas kernels, local(): pl.pallas_call(turn_kernel, name='turn', out_shape=(jax.ShapeDtypeStruct(...  1.47 us

profile of v11, /device:TPU:1, one launch (start us, length us, event | category | flops | bytes accessed | tf_op | source)
XLA Modules:
  0.0 50.7 jit_solution(6702271544933854576)
XLA Ops:
  0.6 48.6 %cg_step.1.result = f32[64,128]{1,0:T(8,128)} custom-call(bf16[64,64]{1,0:T(8,128)(2,1)} %feat_hbm.1, f32[1,64]{1,0:T(1,128)} %bitcast.2, s32[1,64]{1,0:T(1,128)} %bitcast.3, f32[32,64]{1,0:T(8,128)} %sol_hbm.1, f32[32,64]{1,0:T(8,128)} %res_hbm.1, f32[32,64]{1,0:T(8,128)} %dir_hbm.1), custom_call_target="tpu_custom_call" | custom-call | tf_op jit(solution)/shard_map/cg_step/pallas_call | solution.py:488
  49.2 1.5 %turn.1 = (f32[32,64]{1,0:T(8,128)}, f32[32,64]{1,0:T(8,128)}, f32[32,64]{1,0:T(8,128)}, f32[32,64]{1,0:T(8,128)}) custom-call(f32[64,128]{1,0:T(8,128)} %cg_step.1.result), custom_call_target="tpu_custom_call" | custom-call | tf_op jit(solution)/shard_map/turn/pallas_call | solution.py:499
